TPU v7x, 512 devices: a whole 4x8x8 slice. The times are simulated.
512 devices in a mesh: section: 16 (over y, core), dp: 32 (over x, z).
Axes of the slice: x: 4, y: 8, z: 8, core: 2. Of those that a mesh axis runs over, the one named last changes fastest.
Arguments:
- hidden_in: bfloat16 [16, 4096, 8192], P('section', 'dp'), may hold values from -50 to 50
- key_grad: bfloat16 [16, 4096, 1024], P('section', 'dp'), may hold values from -6 to 6
- key_weight: bfloat16 [16, 8192, 1024], P('section', 'dp'), may hold values from -0.1875 to 0.1875
- adapter_a: bfloat16 [16, 64, 8192], P('section', None, 'dp'), may hold values from -0.75 to 0.75
- adapter_b: bfloat16 [16, 64, 1024], P('section'), may hold values from -0.1875 to 0.1875
- norm_gain: float32 [16, 8192], P('section'), may hold values from 0.1 to 1.9
- keep_flags: int32 [16], P('section'), may hold values from 0 to 1, as said below
- valid_counts: int32 [32], P('dp'), may hold values from 32 to 128, as said below
Outputs:
- grad_stream: bfloat16 [16, 4096, 8192], P('section', 'dp')
- grad_adapter_a: float32 [16, 64, 8192], P('section', None, 'dp')
- grad_adapter_b: float32 [16, 64, 1024], P('section', None, 'dp')
Inputs may be any that keep to these rules, and one draw needn't show every extreme that they name: `keep_flags`: some kept layer has the layer 8 positions away (cyclically) dropped. `valid_counts`: the first that many rows of a replica are live; at least one replica has all 128 live.
All inputs are finite; a program needn't handle non-finite values.
Results may differ from a plain program's by a relative error of at most 0.02.
Values may be sent and summed in bfloat16 or wider, within the bound.
No kernel may reach another device: no remote copies, remote signals or barrier semaphores. Data moves between devices by JAX's collectives and lax.ppermute only.
A program may use at most 128 MiB of HBM per device.

v0:
```python
import math

import jax
import jax.numpy as jnp
from jax import lax
from jax.sharding import PartitionSpec as P

ADAPTER_SCALING = 0.5
EPS = 1e-06


def prefix(value, axis, combine, identity):
    length, index = (lax.axis_size(axis), lax.axis_index(axis))
    everything = lax.all_gather(value, axis)
    start = jnp.broadcast_to(jnp.asarray(identity, value.dtype), value.shape)

    def step(k, before):
        at = length - 1 - k
        reached = at > index
        new = combine(before, everything[at])
        return jnp.where(reached, new, before)

    return lax.fori_loop(0, length, step, start)


def contract_final_axis(left, right):
    return lax.dot_general(
        left, right, (((1,), (1,)), ((), ())), preferred_element_type=jnp.float32
    )


def contract_first(left, right):
    return lax.dot_general(
        left, right, (((0,), (0,)), ((), ())), preferred_element_type=jnp.float32
    )


def add_chain(earlier, later):
    return (earlier.astype(jnp.float32) + later.astype(jnp.float32)).astype(jnp.bfloat16)


def column_block(collected_rows, lowrank_cols, weight_portion, a_portion):
    return (
        contract_final_axis(collected_rows, weight_portion)
        + ADAPTER_SCALING * contract_first(lowrank_cols, a_portion)
    ).astype(jnp.bfloat16)


def shards(
    hidden_in, key_grad, key_weight, adapter_a, adapter_b, norm_gain, keep_flags, valid_counts
):
    token_rows = hidden_in.shape[1]
    model_width = hidden_in.shape[2]
    replica_count = lax.axis_size("dp")
    member = lax.axis_index("dp")
    col_share = model_width // replica_count
    scale_factor = ADAPTER_SCALING / math.sqrt(token_rows * replica_count)
    positions = lax.broadcasted_iota(jnp.int32, (token_rows, 1), 0)
    me_kept = keep_flags[0] > 0
    live_rows = (positions < valid_counts[0]) & me_kept
    masked_gradient = jnp.where(live_rows, key_grad[0], jnp.zeros_like(key_grad[0]))
    gain_row = norm_gain[0]
    weight_rows = key_weight[0]
    a_cols = adapter_a[0]
    b_mat = adapter_b[0]
    collected_rows, a_full = (
        lax.all_gather(masked_gradient, "dp", axis=0, tiled=True),
        lax.all_gather(a_cols, "dp", axis=1, tiled=True),
    )
    all_rows = collected_rows.shape[0]
    lowrank_cols = contract_final_axis(b_mat, collected_rows).astype(jnp.bfloat16)
    own_low = jnp.where(me_kept, lowrank_cols, jnp.zeros_like(lowrank_cols))

    def whole_part(operands):
        return column_block(operands[0], operands[1], weight_rows, a_cols)

    def skip_whole(operands):
        return jnp.zeros((all_rows, col_share), jnp.bfloat16)

    dnorm_cols = lax.cond(me_kept, whole_part, skip_whole, (collected_rows, lowrank_cols))
    dnorm_rows = lax.all_to_all(dnorm_cols, "dp", split_axis=0, concat_axis=1, tiled=True)
    resid = hidden_in[0].astype(jnp.float32)
    inv_rms = lax.rsqrt(jnp.mean(resid * resid, axis=1, keepdims=True) + EPS)
    normed = (resid * inv_rms * gain_row).astype(jnp.bfloat16)
    slope_rows = gain_row * dnorm_rows.astype(jnp.float32)
    inner_mean = jnp.mean(resid * slope_rows, axis=1, keepdims=True)
    grad_term = (inv_rms * (slope_rows - resid * inv_rms * inv_rms * inner_mean)).astype(
        jnp.bfloat16
    )
    projected_cols = contract_final_axis(a_full, normed).astype(jnp.bfloat16)
    mine_low = lax.dynamic_slice_in_dim(own_low, member * token_rows, token_rows, 1)
    term_a = scale_factor * jnp.dot(mine_low, normed, preferred_element_type=jnp.float32)
    term_b = scale_factor * jnp.dot(
        projected_cols, masked_gradient, preferred_element_type=jnp.float32
    )
    grad_a, grad_b = (
        lax.psum_scatter(term_a.astype(jnp.bfloat16), "dp", scatter_dimension=1, tiled=True).astype(
            jnp.float32
        ),
        lax.psum_scatter(term_b.astype(jnp.bfloat16), "dp", scatter_dimension=1, tiled=True).astype(
            jnp.float32
        ),
    )
    above = prefix(grad_term, "section", add_chain, jnp.zeros_like(grad_term))
    stream = add_chain(above, grad_term)
    return (stream[None], grad_a[None], grad_b[None])


def solution(mesh):
    return jax.shard_map(
        shards,
        mesh=mesh,
        in_specs=(
            P("section", "dp", None),
            P("section", "dp", None),
            P("section", "dp", None),
            P("section", None, "dp"),
            P("section", None, None),
            P("section", None),
            P("section"),
            P("dp"),
        ),
        out_specs=(P("section", "dp", None), P("section", None, "dp"), P("section", None, "dp")),
        check_vma=False,
    )
```

profile of v0, /device:TPU:1, one launch (start us, length us, event | category | flops | bytes accessed | tf_op | source)
XLA Modules:
  0.0 913.0 jit_solution(10477768845925933015)
XLA Ops:
  10.4 110.5 %all-gather.5.cloned.1.call-done = bf16[4096,1024]{1,0:T(8,128)(2,1)} async-done(((bf16[128,1024]{1,0:T(8,128)(2,1)}), bf16[4096,1024]{1,0:T(8,128)(2,1)}) %all-gather.5.cloned.1.call-update) | async-done | bytes 8388624 | tf_op jit(solution)/shard_map/all_gather | solution.py:67
  120.8 6.0 fusion.12
  126.9 7.9 conditional.1
  126.9 5.8 fusion.2
  134.7 5.3 all-to-all-start
  140.9 3.2 copy.13
  144.1 46.4 %all-to-all-done = bf16[32,128,256]{2,1,0:T(8,128)(2,1)} async-done(((bf16[32,128,256]{2,1,0:T(8,128)(2,1)}), bf16[32,128,256]{2,1,0:T(8,128)(2,1)}, u32[]{:S(2)}, u32[]{:S(2)}) %all-to-all-start) | async-done | bytes 2097184 | tf_op jit(solution)/shard_map/all_to_all | solution.py:81
  190.5 4.1 copy.14
  197.0 28.4 %all-gather.9.cloned.1.call-done = bf16[1,64,8192]{2,1,0:T(8,128)(2,1)} async-done(((bf16[1,64,256]{2,1,0:T(8,128)(2,1)}), bf16[1,64,8192]{2,1,0:T(8,128)(2,1)}) %all-gather.9.cloned.1.call-update) | async-done | bytes 1048592 | tf_op jit(solution)/shard_map/all_gather | solution.py:68
  225.5 3.6 fusion.26
  233.9 4.4 fusion.24
  238.3 4.1 copy.15
  242.5 205.0 %reduce-scatter.5.cloned.1.call-done = bf16[64,32]{0,1:T(8,128)(2,1)} async-done(((bf16[64,1024]{0,1:T(8,128)(2,1)}), bf16[64,32]{0,1:T(8,128)(2,1)}) %reduce-scatter.5.cloned.1.call-update) | async-done | bytes 4112 | tf_op jit(solution)/shard_map/reduce_scatter | solution.py:100
  448.8 221.6 %reduce-scatter.3.cloned.1.call-done = bf16[64,256]{1,0:T(8,128)(2,1)} async-done(((bf16[64,8192]{1,0:T(8,128)(2,1)}), bf16[64,256]{1,0:T(8,128)(2,1)}) %reduce-scatter.3.cloned.1.call-update) | async-done | bytes 32784 | tf_op jit(solution)/shard_map/reduce_scatter | solution.py:97
  671.7 181.0 %all-gather.7.cloned.1.call-done = bf16[16,128,8192]{2,1,0:T(8,128)(2,1)} async-done(((bf16[1,128,8192]{2,1,0:T(8,128)(2,1)}), bf16[16,128,8192]{2,1,0:T(8,128)(2,1)}) %all-gather.7.cloned.1.call-update) | async-done | bytes 33554448 | tf_op jit(solution)/shard_map/all_gather | solution.py:14
  852.7 44.7 %while.16 = (s32[]{:T(128)}, bf16[128,8192]{1,0:T(8,128)(2,1)S(1)}, s32[]{:T(128)}, bf16[16,128,8192]{2,1,0:T(8,128)(2,1)}, s32[]{:T(128)}, /*index=5*/s32[]{:T(128)}, s32[]{:T(128)}, s32[]{:T(128)}) while((s32[]{:T(128)}, bf16[128,8192]{1,0:T(8,128)(2,1)S(1)}, s32[]{:T(128)}, bf16[16,128,8192]{2,1,0:T(8,128)(2,1)}, s32[]{:T(128)}, ...), condition=%wide.region_5.6_spmd.clone, body=%wide.region_4.5_spmd.clone.sunk | while | flops 6291464 | bytes 6291619 | solution.py:23
  855.5 2.8 fusion.43
  861.1 2.8 fusion.43
  866.7 2.8 fusion.43
  869.5 2.8 fusion.43
  875.1 2.8 fusion.43
  880.7 2.8 fusion.43
  899.9 3.7 fusion.25
  903.6 2.9 copy.17
  (46 shorter events, 44.8 us)
Async XLA Ops:
  7.2 113.7 %copy-start = (bf16[1,64,1024]{2,1,0:T(8,128)(2,1)S(1)}, bf16[1,64,1024]{2,1,0:T(8,128)(2,1)}, u32[]{:S(2)}) copy-start(bf16[1,64,1024]{2,1,0:T(8,128)(2,1)} %param.16) | copy-start | bytes 393220
  7.2 113.6 %all-gather.5.cloned.1.call-start = ((), (), s32[]{:S(2)}) async-start(), calls=%async_computation.3 | async-start | bytes 8650752 | tf_op jit(solution)/shard_map/all_gather | solution.py:67
  10.3 116.5 %copy-start.5 = (bf16[1,64,256]{2,1,0:T(8,128)(2,1)S(1)}, bf16[1,64,256]{2,1,0:T(8,128)(2,1)}, u32[]{:S(2)}) copy-start(bf16[1,64,256]{2,1,0:T(8,128)(2,1)} %param.15) | copy-start | bytes 98308
  10.4 116.5 %copy-start.6 = (bf16[1,256,1024]{2,1,0:T(8,128)(2,1)S(1)}, bf16[1,256,1024]{2,1,0:T(8,128)(2,1)}, u32[]{:S(2)}) copy-start(bf16[1,256,1024]{2,1,0:T(8,128)(2,1)} %param.14) | copy-start | bytes 1572868
  134.7 55.7 %all-to-all-start = ((bf16[32,128,256]{2,1,0:T(8,128)(2,1)}), bf16[32,128,256]{2,1,0:T(8,128)(2,1)}, u32[]{:S(2)}, u32[]{:S(2)}) async-start(bf16[32,128,256]{2,1,0:T(8,128)(2,1)} %bitcast.9), calls=%async_computation | async-start | bytes 4194304 | tf_op jit(solution)/shard_map/all_to_all | solution.py:81
  140.1 85.4 %all-gather.9.cloned.1.call-start = ((), (), s32[]{:S(2)}) async-start(), calls=%async_computation.7 | async-start | bytes 1081344 | tf_op jit(solution)/shard_map/all_gather | solution.py:68
  140.8 306.7 %reduce-scatter.5.cloned.1.call-start = ((), (), s32[]{:S(2)}) async-start(), calls=%async_computation.6 | async-start | bytes 270336 | tf_op jit(solution)/shard_map/reduce_scatter | solution.py:100
  140.9 53.7 %copy-start.4 = (f32[1,8192]{1,0:T(1,128)S(1)}, f32[1,8192]{1,0:T(1,128)}, u32[]{:S(2)}) copy-start(f32[1,8192]{1,0:T(1,128)} %param.17) | copy-start | bytes 98308
  144.1 89.8 %copy-start.2 = (bf16[1,128,8192]{1,2,0:T(8,128)(2,1)}, bf16[1,128,8192]{1,2,0:T(8,128)(2,1)S(1)}, u32[]{:S(2)}) copy-start(bf16[1,128,8192]{1,2,0:T(8,128)(2,1)S(1)} %copy.13) | copy-start | bytes 6291460
  144.1 81.4 %copy-start.3 = (bf16[128,1024]{1,0:T(8,128)(2,1)S(1)}, bf16[128,1024]{1,0:T(8,128)(2,1)}, u32[]{:S(2)}) copy-start(bf16[128,1024]{1,0:T(8,128)(2,1)} %bitcast_select_fusion) | copy-start | bytes 786436
  229.1 441.2 %reduce-scatter.3.cloned.1.call-start = ((), (), s32[]{:S(2)}) async-start(), calls=%async_computation.5 | async-start | bytes 1081344 | tf_op jit(solution)/shard_map/reduce_scatter | solution.py:97
  231.6 621.1 %all-gather.7.cloned.1.call-start = ((), (), s32[]{:S(2)}) async-start(), calls=%async_computation.4 | async-start | bytes 35651584 | tf_op jit(solution)/shard_map/all_gather | solution.py:14
  899.9 6.6 copy-start.1
Sparse Core Ops, SparseCore 0:
  11.2 109.5 all-gather.4
  143.9 81.4 all-gather.8
  229.9 217.5 reduce-scatter.4
  452.3 217.9 reduce-scatter.2
  672.5 180.1 all-gather.6
where the time goes:
time: 914 us; the launch traced here: 913 us
  waiting for transfers between devices  794 us (87%)
  other arithmetic  61.3 us (7%)
  matrix products  19.9 us (2%)
  local copies, waits for them, and re-layouts  16.8 us (2%)
  between operations  15.3 us (2%)
    reduce_scatter x1, waiting for transfers between devices, shards(): lax.psum_scatter(term_a.astype(jnp.bfloat16), 'dp', scatter_dimension=1,...  222 us
    reduce_scatter x1, waiting for transfers between devices, shards(): lax.psum_scatter(term_b.astype(jnp.bfloat16), 'dp', scatter_dimension=1,...  205 us
    all_gather x1, waiting for transfers between devices, prefix(): everything = lax.all_gather(value, axis)  181 us
    all_gather x1, waiting for transfers between devices, shards(): lax.all_gather(masked_gradient, 'dp', axis=0, tiled=True)  110 us
    all_to_all x1, waiting for transfers between devices, shards(): lax.all_to_all(dnorm_cols, 'dp', split_axis=0, concat_axis=1, tiled=True)  46.4 us
    select_n x16, other arithmetic, step(): return jnp.where(reached, new, before)  44.2 us
    all_gather x1, waiting for transfers between devices, shards(): lax.all_gather(a_cols, 'dp', axis=1, tiled=True)  28.4 us
  transfers between devices with their start and end apart: 6, of which 6 were waited for; matrix products, arithmetic and copies ran while one was open for 3% of the time, Pallas kernels for 0%

commit v1 on v0

v1 whole, which is shorter than its diff:
```python
import math

import jax
import jax.numpy as jnp
from jax import lax
from jax.sharding import Mesh
from jax.sharding import PartitionSpec as P

ADAPTER_SCALING = 0.5
EPS = 1e-06
F32 = jnp.float32
BF16 = jnp.bfloat16


def contract(left, right, dims):
    return lax.dot_general(left, right, ((dims[:1], dims[1:]), ((), ())), preferred_element_type=F32)


def exchange(value, axes):
    return lax.all_to_all(value, axes, 0, 0, tiled=True)


def inverse_rms(rows):
    return lax.rsqrt(jnp.mean(rows * rows, axis=-1, keepdims=True) + EPS)


def shards(hidden_in, key_grad, key_weight, adapter_a, adapter_b, norm_gain, keep_flags, valid_counts):
    tokens, width = hidden_in.shape[1:]
    key_width = key_grad.shape[2]
    rank = adapter_a.shape[1]
    chips_y, cores = lax.axis_size("y"), lax.axis_size("core")
    nx, nz = lax.axis_size("x"), lax.axis_size("z")
    replicas = nx * nz
    half = tokens // cores
    col_share = width // replicas
    x_cols = width // nx
    scale_factor = ADAPTER_SCALING / math.sqrt(tokens * replicas)

    weight = (
        key_weight[0].astype(F32) + ADAPTER_SCALING * contract(adapter_a[0], adapter_b[0], (0, 0))
    ).astype(BF16)
    weight_z = lax.all_gather(weight, "z", axis=0, tiled=True)

    positions = lax.broadcasted_iota(jnp.int32, (tokens, 1), 0)
    live = (positions < valid_counts[0]) & (keep_flags[0] > 0)
    masked = jnp.where(live, key_grad[0], jnp.zeros_like(key_grad[0]))
    masked_x = exchange(jnp.broadcast_to(masked[None], (nx, tokens, key_width)), "x")
    masked_x = masked_x.reshape(nx, cores, half, key_width).transpose(1, 0, 2, 3)
    masked_x = masked_x.reshape(nx * tokens, key_width)

    hidden_pair = exchange(hidden_in[0].reshape(cores, half, width), "core").astype(F32)
    gain_pair = lax.all_gather(norm_gain, "core", axis=0, tiled=True)[:, None, :]
    inv_pair = inverse_rms(hidden_pair)

    resid = hidden_in[0].astype(F32)
    normed = (resid * inverse_rms(resid) * norm_gain).astype(BF16)
    lowrank = contract(masked, adapter_b[0], (1, 1)).astype(BF16)
    part_a = (scale_factor * contract(lowrank, normed, (0, 0))).astype(BF16)
    part_a = part_a.reshape(rank, replicas, col_share).transpose(1, 0, 2)

    a_z = lax.all_gather(adapter_a, "z", axis=0, tiled=True)
    a_full = lax.all_gather(a_z, "x", axis=0, tiled=True)
    a_full = a_full.transpose(1, 0, 2).reshape(rank, width)
    projected = contract(normed, a_full, (1, 1)).astype(BF16)
    part_b = (scale_factor * contract(projected, masked, (0, 0))).astype(BF16)
    part_b = part_b.reshape(rank, replicas, key_width // replicas).transpose(1, 0, 2)
    part_b = part_b.reshape(replicas, -1, col_share)
    parts = exchange(jnp.concatenate([part_a, part_b], axis=1), ("x", "z"))
    summed = jnp.sum(parts.astype(F32), axis=0)
    grad_a = summed[:rank]
    grad_b = summed[rank:].reshape(rank, key_width // replicas)

    dnorm = contract(masked_x, weight_z, (1, 1)).astype(BF16)
    dnorm = exchange(dnorm.reshape(cores * nx, half, x_cols), ("core", "x"))
    dnorm = dnorm.reshape(cores, nx, half, x_cols).transpose(0, 2, 1, 3).reshape(cores, half, width)
    slope = gain_pair * dnorm.astype(F32)
    inner = jnp.mean(hidden_pair * slope, axis=-1, keepdims=True)
    term = (inv_pair * (slope - hidden_pair * inv_pair * inv_pair * inner)).astype(BF16)

    upper, lower = term[1].astype(F32), term[0].astype(F32)
    total = (upper + lower).astype(BF16)
    slices = exchange(total.reshape(chips_y, half // chips_y, width), "y").astype(F32)
    running = jnp.zeros_like(slices[0])
    above = [None] * chips_y
    for chip in reversed(range(chips_y)):
        above[chip] = running.astype(BF16)
        running = running + slices[chip]
    above = exchange(jnp.stack(above), "y").reshape(half, width).astype(F32)
    stream_upper = (above + upper).astype(BF16)
    stream_lower = (stream_upper.astype(F32) + lower).astype(BF16)
    stream = exchange(jnp.stack([stream_lower, stream_upper]), "core").reshape(tokens, width)
    return stream[None], grad_a[None], grad_b[None]


def solution(mesh):
    sections, replicas = mesh.devices.shape
    split = Mesh(mesh.devices.reshape(sections // 2, 2, 4, replicas // 4), ("y", "core", "x", "z"))
    section, dp = ("y", "core"), ("x", "z")
    return jax.shard_map(
        shards,
        mesh=split,
        in_specs=(
            P(section, dp, None),
            P(section, dp, None),
            P(section, dp, None),
            P(section, None, dp),
            P(section, None, None),
            P(section, None),
            P(section),
            P(dp),
        ),
        out_specs=(P(section, dp, None), P(section, None, dp), P(section, None, dp)),
        check_vma=False,
    )
```

time: 914 us -> 256 us (0.28)
  waiting for transfers between devices: 794 us -> 100 us
  blocking collectives: 0 us -> 53.1 us
  other arithmetic: 61.3 us -> 23.1 us
  starting transfers between devices: 5.69 us -> 27 us
    reduce_scatter x2 -> x0, waiting for transfers between devices: 427 us -> none  [the longest x1 222 us: shards(): lax.psum_scatter(term_a.astype(jnp.bfloat16), 'dp', scatter_dimension=1,...]
    all_gather x3 -> x2, waiting for transfers between devices: 320 us -> 46.5 us  [the longest x1 46.5 us: shards(): weight_z = lax.all_gather(weight, 'z', axis=0, tiled=True)]
    select_n x17 -> x0, other arithmetic: 46 us -> none  [the longest x16 44.2 us: step(): return jnp.where(reached, new, before)]
    all_gather x0 -> x2, blocking collectives: none -> 28.4 us  [the longest x1 21.6 us: shards(): a_z = lax.all_gather(adapter_a, 'z', axis=0, tiled=True)]
    all_to_all x0 -> x2, blocking collectives: none -> 24.8 us  [exchange(): return lax.all_to_all(value, axes, 0, 0, tiled=True)]
    all_to_all x1 -> x5, starting transfers between devices: 5.3 us -> 27 us  [exchange(): return lax.all_to_all(value, axes, 0, 0, tiled=True)]
    all_to_all x1 -> x5, waiting for transfers between devices: 46.4 us -> 53.6 us  [exchange(): return lax.all_to_all(value, axes, 0, 0, tiled=True)]
    dot_general x5 -> x4, matrix products: 19.9 us -> 15.2 us  [contract(): lax.dot_general(left, right, ((dims[:1], dims[1:]), ((), ())), preferred_...]
  transfers between devices with their start and end apart: 6 -> 7, of which waited for: 6 -> 4; matrix products, arithmetic and copies ran while one was open for 3% -> 16% of each run, Pallas kernels for 0% -> 0%
where the time goes in v1:
time: 256 us; the launch traced here: 254 us
  waiting for transfers between devices  100 us (39%)
  blocking collectives  53.1 us (21%)
  starting transfers between devices  27 us (11%)
  other arithmetic  23.1 us (9%)
  local copies, waits for them, and re-layouts  18.1 us (7%)
  between operations  16.9 us (7%)
  matrix products  15.2 us (6%)
    all_to_all x5, waiting for transfers between devices, exchange(): return lax.all_to_all(value, axes, 0, 0, tiled=True)  53.6 us
    all_gather x1, waiting for transfers between devices, shards(): weight_z = lax.all_gather(weight, 'z', axis=0, tiled=True)  46.5 us
    all_to_all x5, starting transfers between devices, exchange(): return lax.all_to_all(value, axes, 0, 0, tiled=True)  27 us
    all_to_all x2, blocking collectives, exchange(): return lax.all_to_all(value, axes, 0, 0, tiled=True)  24.8 us
    all_gather x1, blocking collectives, shards(): a_z = lax.all_gather(adapter_a, 'z', axis=0, tiled=True)  21.6 us
    dot_general x4, matrix products, contract(): lax.dot_general(left, right, ((dims[:1], dims[1:]), ((), ())), preferred_...  15.2 us
    all_gather x1, blocking collectives, shards(): lax.all_gather(norm_gain, 'core', axis=0, tiled=True)[:, None, :]  6.79 us
    unnamed x7, other arithmetic  6.26 us
  transfers between devices with their start and end apart: 7, of which 4 were waited for; matrix products, arithmetic and copies ran while one was open for 16% of the time, Pallas kernels for 0%

profile of v1, /device:TPU:1, one launch (start us, length us, event | category | flops | bytes accessed | tf_op | source)
XLA Modules:
  0.0 253.7 jit_solution(12678289050423778643)
XLA Ops:
  8.9 2.2 fusion.27
  13.6 15.1 %all_to_all.35 = bf16[4,128,1024]{2,1,0:T(8,128)(2,1)S(1)} all-to-all(bf16[4,128,1024]{2,1,0:T(8,128)(2,1)S(1)} %broadcast_in_dim.33), channel_id=1, replica_groups=mesh['y'=8,'core'=2,'x'=4,'z'=8] {'x'}, dimensions={0} | all-to-all | bytes 2097152 | tf_op jit(solution)/shard_map/all_to_all | solution.py:20
  28.8 46.5 %all-gather.4.cloned.1.call-done = bf16[2048,1024]{1,0:T(8,128)(2,1)} async-done(((bf16[256,1024]{1,0:T(8,128)(2,1)}), bf16[2048,1024]{1,0:T(8,128)(2,1)}) %all-gather.4.cloned.1.call-update) | async-done | bytes 4194320 | tf_op jit(solution)/shard_map/all_gather | solution.py:42
  75.3 5.9 %convolution_convert_fusion = bf16[512,2048]{1,0:T(8,128)(2,1)} fusion(bf16[512,1024]{1,0:T(8,128)(2,1)S(1)} %bitcast.93, bf16[2048,1024]{1,0:T(8,128)(2,1)} %all-gather.4.cloned.1.call-done), kind=kOutput, calls=%fused_computation.22 | convolution fusion | flops 2148532224 | bytes 7340032 | tf_op jit(solution)/shard_map/dot_general | solution.py:16
  81.2 5.1 %all-to-all-start.2 = ((bf16[8,64,2048]{2,1,0:T(8,128)(2,1)}), bf16[8,64,2048]{2,1,0:T(8,128)(2,1)S(1)}, u32[]{:S(2)}, u32[]{:S(2)}) async-start(bf16[8,64,2048]{2,1,0:T(8,128)(2,1)} %bitcast.90), calls=%async_computation.2 | async-start | bytes 4194304 | tf_op jit(solution)/shard_map/all_to_all | solution.py:20
  86.2 21.6 %all_gather.14 = bf16[8,64,256]{2,1,0:T(8,128)(2,1)} all-gather(bf16[1,64,256]{2,1,0:T(8,128)(2,1)S(1)} %copy-done.6), channel_id=1, replica_groups=mesh['y'=8,'core'=2,'x'=4,'z'=8] {'z'}, dimensions={0}, use_global_device_ids=true | all-gather | bytes 294912 | tf_op jit(solution)/shard_map/all_gather | solution.py:61
  107.8 6.8 %all-gather = f32[2,1,8192]{2,1,0:T(1,128)S(1)} all-gather(f32[1,1,8192]{2,1,0:T(1,128)S(1)} %bitcast.100), channel_id=1, replica_groups=mesh['y'=8,'core'=2,'x'=4,'z'=8] {'core'}, dimensions={0}, use_global_device_ids=true | all-gather | bytes 98304 | tf_op jit(solution)/shard_map/all_gather | solution.py:52
  116.0 4.1 %all-to-all-start = ((bf16[2,64,8192]{2,1,0:T(8,128)(2,1)}), bf16[2,64,8192]{2,1,0:T(8,128)(2,1)S(1)}, u32[]{:S(2)}, u32[]{:S(2)}) async-start(bf16[2,64,8192]{2,1,0:T(8,128)(2,1)} %bitcast.86), calls=%async_computation | async-start | bytes 4194304 | tf_op jit(solution)/shard_map/all_to_all | solution.py:20
  120.1 2.1 convert_bitcast_fusion.1
  122.2 2.2 copy.34
  124.5 4.1 %fusion.8 = (f32[2,64]{1,0:T(2,128)S(1)}, f32[2,64]{1,0:T(2,128)S(1)}) fusion(bf16[2,64,8192]{2,1,0:T(8,128)(2,1)S(1)} %all-to-all-done, f32[2,64,8192]{2,1,0:T(8,128)} %bitcast.83, f32[2,8192]{1,0:T(2,128)S(1)} %bitcast.96), kind=kLoop, calls=%fused_computation.14 | loop fusion | flops 6291200 | bytes 6358016 | tf_op jit(solution)/shard_map/reduce_sum | solution.py:24
  128.8 2.7 %fusion.13 = bf16[2,64,8192]{2,1,0:T(8,128)(2,1)S(1)} fusion(bf16[2,64,8192]{2,1,0:T(8,128)(2,1)} %copy-done.2, f32[2,64,8192]{2,1,0:T(8,128)S(1)} %bitcast.84, f32[2,64]{1,0:T(2,128)S(1)} %get-tuple-element.19, f32[2,8192]{1,0:T(2,128)S(1)} %bitcast.97, f32[2,64]{1,0:T(2,128)S(1)} %get-tuple-element.18), kind=kLoop, calls=%fused_computation.19 | loop fusion | flops 8388608 | bytes 8455168 | tf_op jit(solution)/shard_map/convert_element_type | solution.py:78
  132.8 6.5 %all-to-all-start.3 = ((bf16[8,8,8192]{2,1,0:T(8,128)(2,1)}), bf16[8,8,8192]{2,1,0:T(8,128)(2,1)S(1)}, u32[]{:S(2)}, u32[]{:S(2)}) async-start(bf16[8,8,8192]{2,1,0:T(8,128)(2,1)} %fusion.34), calls=%async_computation.3 | async-start | bytes 2097152 | tf_op jit(solution)/shard_map/all_to_all | solution.py:20
  141.3 3.5 %fusion = bf16[64,8192]{1,0:T(8,128)(2,1)} fusion(bf16[1,128,8192]{2,1,0:T(8,128)(2,1)} %param.8, f32[8192]{0:T(1024)} %bitcast.98, f32[128]{0:T(128)S(1)} %add_rsqrt_fusion.1, bf16[128,1024]{1,0:T(8,128)(2,1)S(1)} %select_bitcast_fusion, bf16[1,64,1024]{2,1,0:T(8,128)(2,1)S(1)} %copy-done), kind=kOutput, calls=%fused_computation.1 | convolution fusion | flops 156246016 | bytes 3572224 | tf_op jit(solution)/shard_map/dot_general | solution.py:16
  144.8 2.4 copy.38
  147.2 2.3 copy.35
  149.5 3.7 %fusion.28 = bf16[64,1024]{1,0:T(8,128)(2,1)} fusion(bf16[64,8192]{1,0:T(8,128)(2,1)} %bitcast.94, bf16[1,128,8192]{2,1,0:T(8,128)(2,1)} %param.8, f32[8192]{0:T(1024)} %bitcast.99, f32[128]{0:T(128)S(1)} %add_rsqrt_fusion.1, bf16[1,128,1024]{2,1,0:T(8,128)(2,1)S(1)} %copy-done.5, pred[128]{0:T(512)(128)(4,1)S(1)} %compare_and_fusion), kind=kOutput, calls=%fused_computation.42 | convolution fusion | flops 155459584 | bytes 3572352 | tf_op jit(solution)/shard_map/dot_general | solution.py:16
  156.7 2.3 pad_maximum_fusion.1
  159.0 9.5 %all-to-all-done.3 = bf16[8,8,8192]{2,1,0:T(8,128)(2,1)S(1)} async-done(((bf16[8,8,8192]{2,1,0:T(8,128)(2,1)}), bf16[8,8,8192]{2,1,0:T(8,128)(2,1)S(1)}, u32[]{:S(2)}, u32[]{:S(2)}) %all-to-all-start.3) | async-done | bytes 1048608 | tf_op jit(solution)/shard_map/all_to_all | solution.py:20
  169.5 7.1 %all-to-all-start.6 = ((bf16[32,72,256]{2,1,0:T(8,128)(2,1)}), bf16[32,72,256]{2,1,0:T(8,128)(2,1)S(1)}, u32[]{:S(2)}, u32[]{:S(2)}) async-start(bf16[32,72,256]{2,1,0:T(8,128)(2,1)} %pad_maximum_fusion.1), calls=%async_computation.6 | async-start | bytes 2359296 | tf_op jit(solution)/shard_map/all_to_all | solution.py:20
  183.5 20.5 %all-to-all-done.6 = bf16[32,72,256]{2,1,0:T(8,128)(2,1)S(1)} async-done(((bf16[32,72,256]{2,1,0:T(8,128)(2,1)}), bf16[32,72,256]{2,1,0:T(8,128)(2,1)S(1)}, u32[]{:S(2)}, u32[]{:S(2)}) %all-to-all-start.6) | async-done | bytes 1179680 | tf_op jit(solution)/shard_map/all_to_all | solution.py:20
  204.0 4.2 %all-to-all-start.4 = ((bf16[8,8,8192]{2,1,0:T(8,128)(2,1)}), bf16[8,8,8192]{2,1,0:T(8,128)(2,1)}, u32[]{:S(2)}, u32[]{:S(2)}) async-start(bf16[8,8,8192]{2,1,0:T(8,128)(2,1)} %broadcast_dynamic-update-slice_fusion), calls=%async_computation.4 | async-start | bytes 2097152 | tf_op jit(solution)/shard_map/all_to_all | solution.py:20
  209.8 23.5 %all-to-all-done.4 = bf16[8,8,8192]{2,1,0:T(8,128)(2,1)} async-done(((bf16[8,8,8192]{2,1,0:T(8,128)(2,1)}), bf16[8,8,8192]{2,1,0:T(8,128)(2,1)}, u32[]{:S(2)}, u32[]{:S(2)}) %all-to-all-start.4) | async-done | bytes 1048608 | tf_op jit(solution)/shard_map/all_to_all | solution.py:20
  235.3 9.7 %all_to_all.36 = bf16[2,64,8192]{2,1,0:T(8,128)(2,1)S(1)} all-to-all(bf16[2,64,8192]{2,1,0:T(8,128)(2,1)S(1)} %pad_maximum_fusion), channel_id=1, replica_groups=mesh['y'=8,'core'=2,'x'=4,'z'=8] {'core'}, dimensions={0} | all-to-all | bytes 4194304 | tf_op jit(solution)/shard_map/all_to_all | solution.py:20
  (52 shorter events, 23.2 us)
Async XLA Ops:
  8.0 0.9 copy-start
  8.0 67.3 %all-gather.4.cloned.1.call-start = ((), (), s32[]{:S(2)}) async-start(), calls=%async_computation.7 | async-start | bytes 4718592 | tf_op jit(solution)/shard_map/all_gather | solution.py:42
  81.1 5.1 %copy-start.6 = (bf16[1,64,256]{2,1,0:T(8,128)(2,1)S(1)}, bf16[1,64,256]{2,1,0:T(8,128)(2,1)}, u32[]{:S(2)}) copy-start(bf16[1,64,256]{2,1,0:T(8,128)(2,1)} %param.11) | copy-start | bytes 98308
  81.2 26.7 %copy-start.7 = (f32[1,8192]{1,0:T(1,128)S(1)}, f32[1,8192]{1,0:T(1,128)}, u32[]{:S(2)}) copy-start(f32[1,8192]{1,0:T(1,128)} %param.13) | copy-start | bytes 98308
  81.2 33.5 %all-to-all-start.2 = ((bf16[8,64,2048]{2,1,0:T(8,128)(2,1)}), bf16[8,64,2048]{2,1,0:T(8,128)(2,1)S(1)}, u32[]{:S(2)}, u32[]{:S(2)}) async-start(bf16[8,64,2048]{2,1,0:T(8,128)(2,1)} %bitcast.90), calls=%async_computation.2 | async-start | bytes 4194304 | tf_op jit(solution)/shard_map/all_to_all | solution.py:20
  86.2 61.0 %all-gather.6.cloned.1.call-start = ((), (), s32[]{:S(2)}) async-start(), calls=%async_computation.8 | async-start | bytes 1310720 | tf_op jit(solution)/shard_map/all_gather | solution.py:62
  114.7 1.3 copy-start.3
  116.0 8.5 %all-to-all-start = ((bf16[2,64,8192]{2,1,0:T(8,128)(2,1)}), bf16[2,64,8192]{2,1,0:T(8,128)(2,1)S(1)}, u32[]{:S(2)}, u32[]{:S(2)}) async-start(bf16[2,64,8192]{2,1,0:T(8,128)(2,1)} %bitcast.86), calls=%async_computation | async-start | bytes 4194304 | tf_op jit(solution)/shard_map/all_to_all | solution.py:20
  124.5 4.1 %copy-start.2 = (bf16[2,64,8192]{2,1,0:T(8,128)(2,1)}, bf16[2,64,8192]{2,1,0:T(8,128)(2,1)S(1)}, u32[]{:S(2)}) copy-start(bf16[2,64,8192]{2,1,0:T(8,128)(2,1)S(1)} %all-to-all-done) | copy-start | bytes 6291460
  124.5 4.4 %copy-start.1 = (f32[2,4,8,8,2048]{4,3,1,2,0:T(8,128)S(1)}, f32[2,4,8,8,2048]{4,3,1,2,0:T(8,128)}, u32[]{:S(2)}) copy-start(f32[2,4,8,8,2048]{4,3,1,2,0:T(8,128)} %copy.34) | copy-start | bytes 12582916
  132.8 35.8 %all-to-all-start.3 = ((bf16[8,8,8192]{2,1,0:T(8,128)(2,1)}), bf16[8,8,8192]{2,1,0:T(8,128)(2,1)S(1)}, u32[]{:S(2)}, u32[]{:S(2)}) async-start(bf16[8,8,8192]{2,1,0:T(8,128)(2,1)} %fusion.34), calls=%async_computation.3 | async-start | bytes 2097152 | tf_op jit(solution)/shard_map/all_to_all | solution.py:20
  144.8 4.7 %copy-start.5 = (bf16[1,128,1024]{2,1,0:T(8,128)(2,1)S(1)}, bf16[1,128,1024]{2,1,0:T(8,128)(2,1)}, u32[]{:S(2)}) copy-start(bf16[1,128,1024]{2,1,0:T(8,128)(2,1)} %param.9) | copy-start | bytes 786436
  168.5 1.0 copy-start.4
  169.5 34.5 %all-to-all-start.6 = ((bf16[32,72,256]{2,1,0:T(8,128)(2,1)}), bf16[32,72,256]{2,1,0:T(8,128)(2,1)S(1)}, u32[]{:S(2)}, u32[]{:S(2)}) async-start(bf16[32,72,256]{2,1,0:T(8,128)(2,1)} %pad_maximum_fusion.1), calls=%async_computation.6 | async-start | bytes 2359296 | tf_op jit(solution)/shard_map/all_to_all | solution.py:20
  204.0 29.4 %all-to-all-start.4 = ((bf16[8,8,8192]{2,1,0:T(8,128)(2,1)}), bf16[8,8,8192]{2,1,0:T(8,128)(2,1)}, u32[]{:S(2)}, u32[]{:S(2)}) async-start(bf16[8,8,8192]{2,1,0:T(8,128)(2,1)} %broadcast_dynamic-update-slice_fusion), calls=%async_computation.4 | async-start | bytes 2097152 | tf_op jit(solution)/shard_map/all_to_all | solution.py:20
Sparse Core Ops, SparseCore 0:
  11.5 63.7 all-gather.3
Sparse Core Ops, SparseCore 1:
  107.9 30.5 all-gather.5

commit v2 on v1

v2 whole, which is shorter than its diff:
```python
import functools
import math

import jax
import jax.numpy as jnp
from jax import lax
from jax.experimental import pallas as pl
from jax.experimental.pallas import tpu as pltpu
from jax.sharding import Mesh
from jax.sharding import PartitionSpec as P

ADAPTER_SCALING = 0.5
EPS = 1e-06
F32 = jnp.float32
BF16 = jnp.bfloat16
SMEM = pl.BlockSpec(memory_space=pltpu.SMEM)
ANY = pl.BlockSpec(memory_space=pl.ANY)
HBM = pl.BlockSpec(memory_space=pltpu.HBM)


def contract(left, right, dims):
    return lax.dot_general(left, right, ((dims[:1], dims[1:]), ((), ())), preferred_element_type=F32)


def exchange(value, axes):
    return lax.all_to_all(value, axes, 0, 0, tiled=True)


def shift(value, axis, by):
    size = lax.axis_size(axis)
    return lax.ppermute(value, axis, [(i, (i + by) % size) for i in range(size)])


def swap(value, axis, bit):
    return lax.ppermute(value, axis, [(i, i ^ bit) for i in range(lax.axis_size(axis))])


def params(megabytes=12):
    return pltpu.CompilerParams(vmem_limit_bytes=megabytes << 20)


def cost(flops, elements):
    return pl.CostEstimate(flops=flops, bytes_accessed=2 * elements, transcendentals=0)


def in_hbm(value):
    return pltpu.with_memory_space_constraint(value, pltpu.HBM)


def whole(*shape):
    return pl.BlockSpec(shape, lambda *_: (0,) * len(shape))


def fold_kernel(weight_ref, a_ref, b_ref, out_ref):
    rows = weight_ref.shape[0]
    rank, share = a_ref.shape
    low = contract(a_ref[...], b_ref[...], (0, 0))
    out_ref[:rows] = (weight_ref[...].astype(F32) + ADAPTER_SCALING * low).astype(BF16)
    groups = out_ref.shape[1] // share
    depth = rank // groups
    for group in range(groups):
        out_ref[rows:, group * share : (group + 1) * share] = a_ref[group * depth : (group + 1) * depth]


def fold(weight, a_cols, b_mat):
    rows, key_width = weight.shape
    packed = a_cols.size // key_width
    return pl.pallas_call(
        fold_kernel,
        grid=(1,),
        out_shape=jax.ShapeDtypeStruct((rows + packed, key_width), BF16),
        in_specs=[whole(*weight.shape), whole(*a_cols.shape), whole(*b_mat.shape)],
        out_specs=whole(rows + packed, key_width),
        compiler_params=params(),
        cost_estimate=cost(2 * a_cols.shape[0] * weight.size, 3 * weight.size),
        name="fold",
    )(weight, a_cols, b_mat)


def mask_kernel(keep_ref, count_ref, grad_ref, *refs):
    out_ref = refs[-1]
    grad = grad_ref[...]
    positions = lax.broadcasted_iota(jnp.int32, (grad.shape[0], 1), 0)
    limit = jnp.where(keep_ref[0] > 0, count_ref[0], 0)
    out_ref[0] = jnp.where(positions < limit, grad, jnp.zeros_like(grad))


def mask(keep, count, grad, after, copies):
    return pl.pallas_call(
        mask_kernel,
        grid=(copies,),
        out_shape=pltpu.HBM((copies,) + grad.shape, BF16),
        in_specs=[SMEM, SMEM, whole(*grad.shape)] + [ANY] * len(after),
        out_specs=pl.BlockSpec((1,) + grad.shape, lambda i: (i, 0, 0)),
        compiler_params=params(),
        cost_estimate=cost(grad.size, 5 * grad.size),
        name="mask",
    )(keep, count, grad, *after)


def products_kernel(share, count, given, masked_ref, *refs):
    blocks, (out_ref, a_ref) = refs[:count], refs[-2:]
    nx, tokens, key_width = masked_ref.shape
    half = out_ref.shape[1]
    rows = masked_ref[...].reshape(nx * tokens, key_width)
    at = 0
    for block in blocks:
        depth = min(block.shape[0], share)
        columns = contract(rows, block[:depth], (1, 1)).astype(BF16)
        for chip in range(nx):
            for part in range(tokens // half):
                start = chip * tokens + part * half
                out_ref[part * nx + chip, :, at : at + depth] = columns[start : start + half]
        at += depth
    slot = 0
    for ref in refs[count : count + given]:
        a_ref[slot : slot + ref.shape[0]] = ref[...]
        slot += ref.shape[0]
    for block in blocks:
        if block.shape[0] > share:
            a_ref[slot] = block[share:]
            slot += 1


def products(masked_x, blocks, share, cores, width, a_parts=(), column=0, into=None, after=()):
    nx, tokens, key_width = masked_x.shape
    columns = sum(min(block.shape[0], share) for block in blocks)
    shape = (cores * nx, tokens // cores, width)
    extra = list(after) + ([] if into is None else [into])
    slots = sum(part.shape[0] for part in a_parts) + sum(block.shape[0] > share for block in blocks)
    rows = max(block.shape[0] for block in blocks) - share
    return pl.pallas_call(
        functools.partial(products_kernel, share, len(blocks), len(a_parts)),
        grid=(1,),
        out_shape=(pltpu.HBM(shape, BF16), jax.ShapeDtypeStruct((slots, rows, key_width), BF16)),
        in_specs=[whole(*masked_x.shape)]
        + [whole(*value.shape) for value in (*blocks, *a_parts)]
        + [ANY] * len(after)
        + [HBM] * (into is not None),
        out_specs=(
            pl.BlockSpec(shape[:2] + (columns,), lambda i: (0, 0, column // columns)),
            whole(slots, rows, key_width),
        ),
        input_output_aliases={} if into is None else {len(blocks) + len(a_parts) + len(extra): 0},
        compiler_params=params(20),
        cost_estimate=cost(2 * masked_x.size * columns, 2 * masked_x.size),
        name="products",
    )(masked_x, *blocks, *a_parts, *extra)


def term_kernel(share, offsets, nz, place_ref, own_ref, other_ref, gain_ref, *refs):
    pieces, (term_ref, total_ref) = refs[: len(offsets)], refs[-2:]
    rows, width = own_ref.shape
    nx = pieces[0].shape[0] // 2
    z, core = place_ref[0], place_ref[1]

    def places():
        for chip in range(nx):
            for piece, piece_offsets in zip(pieces, offsets):
                for at, offset in enumerate(piece_offsets):
                    slot = lax.rem(z + (offset + nz), nz)
                    start = pl.multiple_of(chip * (nz * share) + slot * share, share)
                    yield chip, piece, slice(at * share, (at + 1) * share), pl.ds(start, share)

    layers = ((own_ref, core), (other_ref, 1 - core))
    factors = []
    for hidden_ref, layer in layers:
        partial = jnp.zeros((rows, share), F32)
        squares = jnp.zeros((rows, share), F32)
        for chip, piece, cols, place in places():
            slope = gain_ref[layer, :, place] * piece[layer * nx + chip, :, cols].astype(F32)
            hidden = hidden_ref[:, place].astype(F32)
            partial += hidden * slope
            squares += hidden * hidden
        inv = lax.rsqrt(jnp.sum(squares, axis=1, keepdims=True) * (1.0 / width) + EPS)
        inner = jnp.sum(partial, axis=1, keepdims=True) * (1.0 / width)
        factors.append((inv, inv * inv * inner))
    for chip, piece, cols, place in places():
        total = None
        for (hidden_ref, layer), (inv, factor) in zip(layers, factors):
            slope = gain_ref[layer, :, place] * piece[layer * nx + chip, :, cols].astype(F32)
            term = (inv * (slope - hidden_ref[:, place].astype(F32) * factor)).astype(BF16)
            term_ref[layer, :, place] = term
            total = term.astype(F32) if total is None else total + term.astype(F32)
        total_ref[:, place] = total.astype(BF16)


def norm_backward(place, hidden, other, gain_pair, pieces, offsets, after, share, nz):
    half, width = other.shape[0] // 2, other.shape[1]
    rows = 16
    steps = half // rows

    def by_rows(array):
        return pl.BlockSpec((array.shape[0], rows, array.shape[2]), lambda i, at: (0, i, 0))

    half_block = pl.BlockSpec((rows, width), lambda i, at: (at[1] * steps + i, 0))
    return pl.pallas_call(
        functools.partial(term_kernel, share, offsets, nz),
        grid_spec=pltpu.PrefetchScalarGridSpec(
            num_scalar_prefetch=1,
            grid=(steps,),
            in_specs=[
                half_block,
                half_block,
                whole(*gain_pair.shape),
            ]
            + [by_rows(piece) for piece in pieces]
            + [ANY] * len(after),
            out_specs=(pl.BlockSpec((2, rows, width), lambda i, at: (0, i, 0)), pl.BlockSpec((rows, width), lambda i, at: (i, 0))),
        ),
        out_shape=(pltpu.HBM((2, half, width), BF16), pltpu.HBM((half, width), BF16)),
        compiler_params=params(),
        cost_estimate=cost(20 * hidden.size, 4 * hidden.size),
        name="norm_backward",
    )(place, hidden, other, gain_pair, *pieces, *after)


def above_kernel(slices_ref, *refs):
    above_ref = refs[-1]
    chips = slices_ref.shape[0]
    running = jnp.zeros(slices_ref.shape[1:], F32)
    for chip in reversed(range(chips)):
        above_ref[chip] = running.astype(BF16)
        if chip:
            running += slices_ref[chip].astype(F32)


def sums_above(slices, after):
    chips, rows, width = slices.shape
    spec = pl.BlockSpec((chips, rows, width // 2), lambda i: (0, 0, i))
    return pl.pallas_call(
        above_kernel,
        grid=(2,),
        out_shape=pltpu.HBM(slices.shape, BF16),
        in_specs=[spec] + [ANY] * len(after),
        out_specs=spec,
        compiler_params=params(),
        cost_estimate=cost(slices.size, 2 * slices.size),
        name="sums_above",
    )(slices, *after)


def normalise_kernel(share, hidden_ref, gain_ref, out_ref):
    tokens, width = hidden_ref.shape
    squares = jnp.zeros((tokens, share), F32)
    for at in range(0, width, share):
        hidden = hidden_ref[:, at : at + share].astype(F32)
        squares += hidden * hidden
    inv = lax.rsqrt(jnp.sum(squares, axis=1, keepdims=True) * (1.0 / width) + EPS)
    for at in range(0, width, share):
        cols = slice(at, at + share)
        chip, place = divmod(at, out_ref.shape[2])
        normed = hidden_ref[:, cols].astype(F32) * inv * gain_ref[:, cols]
        out_ref[chip, :, place : place + share] = normed.astype(BF16)


def normalise(hidden, gain, share, nx):
    tokens, width = hidden.shape
    rows = 64
    return pl.pallas_call(
        functools.partial(normalise_kernel, share),
        grid=(tokens // rows,),
        out_shape=pltpu.HBM((nx, tokens, width // nx), BF16),
        in_specs=[pl.BlockSpec((rows, width), lambda i: (i, 0)), whole(*gain.shape)],
        out_specs=pl.BlockSpec((nx, rows, width // nx), lambda i: (0, i, 0)),
        compiler_params=params(),
        cost_estimate=cost(6 * hidden.size, 2 * hidden.size),
        name="normalise",
    )(hidden, gain)


def partials_kernel(share, offsets, nz, scale_factor, z_ref, masked_ref, normed_ref, a_ref, b_ref, *refs):
    part_ref, projected_ref = refs[-2:]
    nx, tokens, key_width = masked_ref.shape
    lowrank = contract(masked_ref[...].reshape(nx * tokens, key_width), b_ref[...], (1, 1)).astype(BF16)
    for at in range(nz):
        normed = normed_ref[:, :, at * share : (at + 1) * share].reshape(nx * tokens, share)
        part_ref[at] = (scale_factor * contract(lowrank, normed, (0, 0))).astype(BF16)
    total = jnp.zeros(projected_ref.shape, F32)
    for at, offset in enumerate(offsets):
        slot = lax.rem(z_ref[0] + (offset + nz), nz)
        place = pl.ds(pl.multiple_of(slot * share, share), share)
        packed = a_ref[at]
        groups = packed.shape[1] // share
        a_cols = jnp.concatenate([packed[:, g * share : (g + 1) * share] for g in range(groups)], axis=0)
        total += contract(a_cols, normed_ref[:, :, place].reshape(nx * tokens, share), (1, 1))
    projected_ref[...] = total.astype(BF16)


def partials(z, masked_x, normed_x, a_own, b_mat, offsets, after, share, nz, scale_factor):
    nx, tokens, _ = masked_x.shape
    rank = b_mat.shape[0]
    operands = (masked_x, normed_x, a_own, b_mat)
    shapes = ((nz, rank, share), (rank, nx * tokens))
    return pl.pallas_call(
        functools.partial(partials_kernel, share, offsets, nz, scale_factor),
        grid=(1,),
        out_shape=tuple(jax.ShapeDtypeStruct(shape, BF16) for shape in shapes),
        in_specs=[SMEM] + [whole(*operand.shape) for operand in operands] + [HBM] * len(after),
        out_specs=tuple(whole(*shape) for shape in shapes),
        compiler_params=params(16),
        cost_estimate=cost(4 * normed_x.size * rank, 2 * normed_x.size),
        name="partials",
    )(z, *operands, *after)


def partial_b_kernel(scale_factor, x_ref, masked_ref, *refs):
    parts, out_ref = refs[:-1], refs[-1]
    nx, tokens, _ = masked_ref.shape
    share = out_ref.shape[1]
    projected = parts[0][...].astype(F32)
    for part in parts[1:]:
        projected += part[...].astype(F32)
    place = pl.ds(pl.multiple_of(x_ref[0] * share, share), share)
    rows = masked_ref[:, :, place].reshape(nx * tokens, share)
    out_ref[...] = (scale_factor * contract(projected.astype(BF16), rows, (1, 0))).astype(BF16)


def partial_b(x, masked_x, parts, scale_factor):
    nx, _, key_width = masked_x.shape
    shape = (parts[0].shape[0], key_width // nx)
    return pl.pallas_call(
        functools.partial(partial_b_kernel, scale_factor),
        grid=(1,),
        out_shape=jax.ShapeDtypeStruct(shape, BF16),
        in_specs=[SMEM, whole(*masked_x.shape)] + [whole(*part.shape) for part in parts],
        out_specs=whole(*shape),
        compiler_params=params(),
        cost_estimate=cost(2 * masked_x.size * shape[0] // nx, masked_x.size),
        name="partial_b",
    )(x, masked_x, *parts)


def halves_kernel(side_ref, a_ref, b_ref, *refs):
    kept_ref, sent_ref = refs[-2:]
    half = kept_ref.shape[0]
    rank = a_ref.shape[1]
    for at in range(half):
        for out, begin in ((kept_ref, side_ref[0] * half), (sent_ref, (1 - side_ref[0]) * half)):
            out[at, :rank] = a_ref[begin + at]
            out[at, rank:] = b_ref[begin + at]


def halves(part_a, part_b, side, after):
    nz, rank, share = part_a.shape
    shape = (nz // 2, rank + part_b.shape[1], share)
    return pl.pallas_call(
        halves_kernel,
        grid=(1,),
        out_shape=(jax.ShapeDtypeStruct(shape, BF16),) * 2,
        in_specs=[SMEM, whole(*part_a.shape), whole(*part_b.shape)] + [HBM] * len(after),
        out_specs=(whole(*shape),) * 2,
        compiler_params=params(),
        cost_estimate=cost(0, 2 * part_a.size),
        name="halves",
    )(side, part_a, part_b, *after)


def add_kernel(count, side_ref, *refs):
    outs = refs[-1:] if refs[0].shape[0] == 1 else refs[-2:]
    half = outs[0].shape[0]
    for at in range(half):
        for out, begin in zip(outs, (side_ref[0] * half, (1 - side_ref[0]) * half)):
            where = begin + at if len(outs) == 2 else at
            total = refs[0][where].astype(F32)
            for ref in refs[1:count]:
                total += ref[where].astype(F32)
            out[at] = total.astype(out.dtype)


def add(values, side):
    shape = values[0].shape
    single = shape[0] == 1
    half = shape if single else (shape[0] // 2,) + shape[1:]
    out = jax.ShapeDtypeStruct(half, F32 if single else BF16)
    return pl.pallas_call(
        functools.partial(add_kernel, len(values)),
        grid=(1,),
        out_shape=(out,) * (1 if single else 2),
        in_specs=[SMEM] + [whole(*shape)] * len(values),
        out_specs=(whole(*half),) * (1 if single else 2),
        compiler_params=params(),
        cost_estimate=cost(len(values) * values[0].size, 4 * values[0].size),
        name="add",
    )(side, *values)


def scatter_sum(part_a, part_b, axis, after=()):
    bit = lax.axis_size(axis) // 2
    index = lax.axis_index(axis)
    kept, sent = halves(part_a, part_b, ((index // bit) % 2)[None], after)
    while bit > 1:
        received = swap(sent, axis, bit)
        bit //= 2
        kept, sent = add([kept, received], ((index // bit) % 2)[None])
    return add([kept, swap(sent, axis, bit)], index[None])[0][0]


def shards(hidden_in, key_grad, key_weight, adapter_a, adapter_b, norm_gain, keep_flags, valid_counts):
    tokens, width = hidden_in.shape[1:]
    key_width = key_grad.shape[2]
    rank = adapter_a.shape[1]
    chips_y, cores = lax.axis_size("y"), lax.axis_size("core")
    nx, nz = lax.axis_size("x"), lax.axis_size("z")
    replicas = nx * nz
    half = tokens // cores
    share = width // replicas
    scale_factor = ADAPTER_SCALING / math.sqrt(tokens * replicas)
    x_index, z_index, core = (lax.axis_index(axis) for axis in ("x", "z", "core"))

    block = fold(in_hbm(key_weight[0]), in_hbm(adapter_a[0]), in_hbm(adapter_b[0]))
    masked = mask(keep_flags, valid_counts, in_hbm(key_grad[0]), [block], nx)
    masked_x = exchange(masked, "x")
    up, down = [block], [block]
    for step in range(1, nz // 2):
        up.append(shift(up[-1], "z", 1))
        down.append(shift(down[-1], "z", -1))
    up.append(shift(up[-1], "z", 1))

    hidden = in_hbm(hidden_in[0])
    other = in_hbm(swap(hidden, "core", 1))
    gain_pair = lax.all_gather(norm_gain, "core", axis=0, tiled=True)[:, None, :]

    rounds = [
        ([block, up[1], down[1]], [0, -1, 1], 0),
        ([up[2], down[2]], [-2, 2], 4),
        ([up[3], down[3]], [-3, 3], 6),
        ([up[4]], [-4], 3),
    ]
    normed_x = exchange(normalise(hidden, norm_gain, share, nx), "x")
    dnorm, a_own = None, None
    for blocks, _, slot in rounds:
        dnorm, a_own = products(
            masked_x,
            blocks,
            share,
            cores,
            nz * share,
            [] if a_own is None else [a_own],
            column=slot * share,
            into=dnorm,
            after=[normed_x] if slot == 6 else [],
        )
    a_offsets = [offset for _, round_offsets, _ in rounds for offset in round_offsets]
    offsets = [0, -1, 1, -4, -2, 2, -3, 3]
    dnorm = in_hbm(dnorm)
    piece = in_hbm(exchange(dnorm, ("core", "x")))

    part_a, projected = partials(
        z_index[None], masked_x, normed_x, a_own, adapter_b[0], a_offsets, [dnorm], share, nz, scale_factor
    )
    projected = [projected] + [shift(projected, "x", by) for by in (-1, 1, 2)]
    part_b = partial_b(x_index[None], masked_x, projected, scale_factor)
    part_b = part_b.reshape(rank, nz, key_width // replicas).transpose(1, 0, 2).reshape(nz, -1, share)
    term, total = norm_backward(
        jnp.stack([z_index, core]), hidden, other, gain_pair, [piece], [offsets], [part_a], share, nz
    )

    slices = exchange(total.reshape(chips_y, half // chips_y, width), "y")
    above_slices = sums_above(slices, [part_b])
    above = exchange(above_slices, "y").reshape(half, width).astype(F32)
    stream_upper = (above + term[1].astype(F32)).astype(BF16)
    stream_lower = (stream_upper.astype(F32) + term[0].astype(F32)).astype(BF16)
    stream = exchange(jnp.stack([stream_lower, stream_upper]), "core").reshape(tokens, width)
    summed = scatter_sum(part_a, part_b, "z", [above_slices])
    grad_a = summed[:rank]
    grad_b = summed[rank:].reshape(rank, key_width // replicas)
    return stream[None], grad_a[None], grad_b[None]


def solution(mesh):
    sections, replicas = mesh.devices.shape
    split = Mesh(mesh.devices.reshape(sections // 2, 2, 4, replicas // 4), ("y", "core", "x", "z"))
    section, dp = ("y", "core"), ("x", "z")
    return jax.shard_map(
        shards,
        mesh=split,
        in_specs=(
            P(section, dp, None),
            P(section, dp, None),
            P(section, dp, None),
            P(section, None, dp),
            P(section, None, None),
            P(section, None),
            P(section),
            P(dp),
        ),
        out_specs=(P(section, dp, None), P(section, None, dp), P(section, None, dp)),
        check_vma=False,
    )
```

time: 256 us -> 205 us (0.80)
  starting transfers between devices: 27 us -> 75.8 us
  blocking collectives: 53.1 us -> 7.51 us
  Pallas kernels: 0 us -> 28.2 us
  other arithmetic: 23.1 us -> 2.25 us
  waiting for transfers between devices: 100 us -> 81.5 us
  matrix products: 15.2 us -> 0 us
  between operations: 16.9 us -> 2.24 us
  local copies, waits for them, and re-layouts: 18.1 us -> 6.22 us
    ppermute x0 -> x14, starting transfers between devices: none -> 49.6 us  [the longest x10 36.9 us: shift(): lax.ppermute(value, axis, [(i, (i + by) % size) for i in range(size)])]
    all_gather x2 -> x0, waiting for transfers between devices: 46.5 us -> none  [the longest x1 46.5 us: shards(): weight_z = lax.all_gather(weight, 'z', axis=0, tiled=True)]
    ppermute x0 -> x14, waiting for transfers between devices: none -> 43.9 us  [the longest x10 25.2 us: shift(): lax.ppermute(value, axis, [(i, (i + by) % size) for i in range(size)])]
    pallas_call x0 -> x15, Pallas kernels: none -> 28.2 us  [the longest x4 11.1 us: products(): pl.pallas_call(functools.partial(products_kernel, share, len(blocks), len...]
    all_gather x1 -> x0, blocking collectives: 21.6 us -> none  [shards(): a_z = lax.all_gather(adapter_a, 'z', axis=0, tiled=True)]
    all_to_all x2 -> x1, blocking collectives: 24.8 us -> 5.53 us  [exchange(): return lax.all_to_all(value, axes, 0, 0, tiled=True)]
    all_to_all x5, waiting for transfers between devices: 53.6 us -> 37.6 us  [exchange(): return lax.all_to_all(value, axes, 0, 0, tiled=True)]
    dot_general x4 -> x0, matrix products: 15.2 us -> none  [contract(): lax.dot_general(left, right, ((dims[:1], dims[1:]), ((), ())), preferred_...]
  transfers between devices with their start and end apart: 7 -> 19, of which waited for: 4 -> 11; matrix products, arithmetic and copies ran while one was open for 16% -> 1% of each run, Pallas kernels for 0% -> 8%
where the time goes in v2:
time: 205 us; the launch traced here: 204 us
  waiting for transfers between devices  81.5 us (40%)
  starting transfers between devices  75.8 us (37%)
  Pallas kernels  28.2 us (14%)
  blocking collectives  7.51 us (4%)
  local copies, waits for them, and re-layouts  6.22 us (3%)
  other arithmetic  2.25 us (1%)
  between operations  2.24 us (1%)
    all_to_all x5, waiting for transfers between devices, exchange(): return lax.all_to_all(value, axes, 0, 0, tiled=True)  37.6 us
    ppermute x10, starting transfers between devices, shift(): lax.ppermute(value, axis, [(i, (i + by) % size) for i in range(size)])  36.9 us
    all_to_all x5, starting transfers between devices, exchange(): return lax.all_to_all(value, axes, 0, 0, tiled=True)  26.2 us
    ppermute x10, waiting for transfers between devices, shift(): lax.ppermute(value, axis, [(i, (i + by) % size) for i in range(size)])  25.2 us
    ppermute x4, waiting for transfers between devices, swap(): lax.ppermute(value, axis, [(i, i ^ bit) for i in range(lax.axis_size(axis...  18.6 us
    ppermute x4, starting transfers between devices, swap(): lax.ppermute(value, axis, [(i, i ^ bit) for i in range(lax.axis_size(axis...  12.7 us
    pallas_call x4, Pallas kernels, products(): pl.pallas_call(functools.partial(products_kernel, share, len(blocks), len...  11.1 us
    pallas_call x1, Pallas kernels, norm_backward(): pl.pallas_call(functools.partial(term_kernel, share, offsets, nz), grid_s...  5.89 us
  transfers between devices with their start and end apart: 19, of which 11 were waited for; matrix products, arithmetic and copies ran while one was open for 1% of the time, Pallas kernels for 8%

profile of v2, /device:TPU:1, one launch (start us, length us, event | category | flops | bytes accessed | tf_op | source)
XLA Modules:
  0.0 203.6 jit_solution(7352001663353754519)
XLA Ops:
  6.7 4.8 %all-to-all-start = ((bf16[4,128,1024]{2,1,0:T(8,128)(2,1)}), bf16[4,128,1024]{2,1,0:T(8,128)(2,1)S(1)}, u32[]{:S(2)}, u32[]{:S(2)}) async-start(bf16[4,128,1024]{2,1,0:T(8,128)(2,1)} %mask.1), calls=%async_computation | async-start | bytes 2097152 | tf_op jit(solution)/shard_map/all_to_all | solution.py:26
  11.5 4.0 %collective-permute-start.1 = (bf16[272,1024]{1,0:T(8,128)(2,1)}, bf16[272,1024]{1,0:T(8,128)(2,1)}, u32[]{:S(2)}, u32[]{:S(2)}) collective-permute-start(bf16[272,1024]{1,0:T(8,128)(2,1)} %fold.1.refs_0_), channel_id=1, source_target_pairs={{0,1},{1,2},{2,3},{3,4},{4,5},{5,6},{6,7},{7,0},{8,9},{9,10},{10,1... | collective-permute-start | bytes 1671176 | tf_op jit(solution)/shard_map/ppermute | solution.py:31
  15.5 8.6 %collective-permute-start.5 = (bf16[272,1024]{1,0:T(8,128)(2,1)}, bf16[272,1024]{1,0:T(8,128)(2,1)}, u32[]{:S(2)}, u32[]{:S(2)}) collective-permute-start(bf16[272,1024]{1,0:T(8,128)(2,1)} %fold.1.refs_0_), channel_id=1, source_target_pairs={{0,7},{1,0},{2,1},{3,2},{4,3},{5,4},{6,5},{7,6},{8,15},{9,8},{10,9... | collective-permute-start | bytes 1671176 | tf_op jit(solution)/shard_map/ppermute | solution.py:31
  24.1 10.4 %collective-permute-done.1.refs_1_ = bf16[272,1024]{1,0:T(8,128)(2,1)} collective-permute-done((bf16[272,1024]{1,0:T(8,128)(2,1)}, bf16[272,1024]{1,0:T(8,128)(2,1)}, u32[]{:S(2)}, u32[]{:S(2)}) %collective-permute-start.1) | collective-permute-done | bytes 557088 | tf_op jit(solution)/shard_map/ppermute | solution.py:31
  36.5 3.1 %normalise.1 = bf16[4,128,2048]{2,1,0:T(8,128)(2,1)} custom-call(bf16[128,8192]{1,0:T(8,128)(2,1)} %bitcast.24, f32[1,8192]{1,0:T(1,128)S(1)} %copy-done.5), custom_call_target="tpu_custom_call" | custom-call | flops 6291456 | bytes 4194304 | tf_op jit(solution)/shard_map/normalise/pallas_call | solution.py:260
  39.6 3.9 %all-to-all-start.1 = ((bf16[4,128,2048]{2,1,0:T(8,128)(2,1)}), bf16[4,128,2048]{2,1,0:T(8,128)(2,1)S(1)}, u32[]{:S(2)}, u32[]{:S(2)}) async-start(bf16[4,128,2048]{2,1,0:T(8,128)(2,1)} %normalise.1), calls=%async_computation.1 | async-start | bytes 4194304 | tf_op jit(solution)/shard_map/all_to_all | solution.py:26
  43.5 4.6 %collective-permute-start.6 = (bf16[272,1024]{1,0:T(8,128)(2,1)}, bf16[272,1024]{1,0:T(8,128)(2,1)}, u32[]{:S(2)}, u32[]{:S(2)}) collective-permute-start(bf16[272,1024]{1,0:T(8,128)(2,1)} %collective-permute-done.5.refs_2_), channel_id=1, source_target_pairs={{0,7},{1,0},{2,1},{3,2},{4,3},{5,4},{6,5},{7,6},{8,15},{9,8},{10,9... | collective-permute-start | bytes 1671176 | tf_op jit(solution)/shard_map/ppermute | solution.py:31
  52.4 5.4 %collective-permute-done.6.refs_1_ = bf16[272,1024]{1,0:T(8,128)(2,1)} collective-permute-done((bf16[272,1024]{1,0:T(8,128)(2,1)}, bf16[272,1024]{1,0:T(8,128)(2,1)}, u32[]{:S(2)}, u32[]{:S(2)}) %collective-permute-start.6) | collective-permute-done | bytes 557088 | tf_op jit(solution)/shard_map/ppermute | solution.py:31
  57.9 5.3 %collective-permute-start.7 = (bf16[272,1024]{1,0:T(8,128)(2,1)}, bf16[272,1024]{1,0:T(8,128)(2,1)}, u32[]{:S(2)}, u32[]{:S(2)}) collective-permute-start(bf16[272,1024]{1,0:T(8,128)(2,1)} %collective-permute-done.6.refs_1_), channel_id=1, source_target_pairs={{0,7},{1,0},{2,1},{3,2},{4,3},{5,4},{6,5},{7,6},{8,15},{9,8},{10,9... | collective-permute-start | bytes 1671176 | tf_op jit(solution)/shard_map/ppermute | solution.py:31
  67.5 5.3 %collective-permute-start = (bf16[128,8192]{1,0:T(8,128)(2,1)}, bf16[128,8192]{1,0:T(8,128)(2,1)}, u32[]{:S(2)}, u32[]{:S(2)}) collective-permute-start(bf16[128,8192]{1,0:T(8,128)(2,1)} %bitcast.25), channel_id=1, source_target_pairs={{0,32},{32,0},{1,33},{33,1},{2,34},{34,2},{3,35},{35,3},{4,36},{36... | collective-permute-start | bytes 6291464 | tf_op jit(solution)/shard_map/ppermute | solution.py:35
  72.8 3.3 %products.4 = (bf16[8,64,2048]{2,1,0:T(8,128)(2,1)}, bf16[3,16,1024]{2,1,0:T(8,128)(2,1)S(1)}) custom-call(bf16[4,128,1024]{2,1,0:T(8,128)(2,1)S(1)} %all-to-all-done.masked_ref, bf16[272,1024]{1,0:T(8,128)(2,1)} %fold.1.refs_0_, bf16[272,1024]{1,0:T(8,128)(2,1)} %collective-permute-done.1.refs_1_, bf16[272,1024]{1,0:T(8,128)(2,1)} %collective-permute-done.5.refs_2_), custom_call_target="tpu_custom_call" | custom-call | flops 805306368 | bytes 2097152 | tf_op jit(solution)/shard_map/products/pallas_call | solution.py:132
  84.6 6.8 %all-to-all-start.2 = ((bf16[8,64,2048]{2,1,0:T(8,128)(2,1)}), bf16[8,64,2048]{2,1,0:T(8,128)(2,1)}, u32[]{:S(2)}, u32[]{:S(2)}) async-start(bf16[8,64,2048]{2,1,0:T(8,128)(2,1)} %get-tuple-element.27.refs_0_), calls=%async_computation.2 | async-start | bytes 4194304 | tf_op jit(solution)/shard_map/all_to_all | solution.py:26
  96.9 20.8 %all-to-all-done.2.refs_0_ = bf16[8,64,2048]{2,1,0:T(8,128)(2,1)} async-done(((bf16[8,64,2048]{2,1,0:T(8,128)(2,1)}), bf16[8,64,2048]{2,1,0:T(8,128)(2,1)}, u32[]{:S(2)}, u32[]{:S(2)}) %all-to-all-start.2) | async-done | bytes 2097184 | tf_op jit(solution)/shard_map/all_to_all | solution.py:26
  118.5 5.9 %norm_backward.1 = (bf16[2,64,8192]{2,1,0:T(8,128)(2,1)}, bf16[64,8192]{1,0:T(8,128)(2,1)}) custom-call(s32[2]{0:T(128)S(1)} %pad_add_fusion.place_ref, bf16[128,8192]{1,0:T(8,128)(2,1)} %bitcast.26, bf16[128,8192]{1,0:T(8,128)(2,1)} %collective-permute-done.other_ref, f32[2,1,8192]{2,1,0:T(1,128)S(1)} %copy-done.2, ...), custom_call_target="tpu_custom_call" | custom-call | flops 20971520 | bytes 8388608 | tf_op jit(solution)/shard_map/norm_backward/pallas_call | solution.py:197
  124.4 6.9 %all-to-all-start.3 = ((bf16[8,8,8192]{2,1,0:T(8,128)(2,1)}), bf16[8,8,8192]{2,1,0:T(8,128)(2,1)S(1)}, u32[]{:S(2)}, u32[]{:S(2)}) async-start(bf16[8,8,8192]{2,1,0:T(8,128)(2,1)} %bitcast.28), calls=%async_computation.3 | async-start | bytes 2097152 | tf_op jit(solution)/shard_map/all_to_all | solution.py:26
  133.9 4.3 %collective-permute-start.8 = (bf16[64,512]{1,0:T(8,128)(2,1)S(1)}, bf16[64,512]{1,0:T(8,128)(2,1)S(1)}, u32[]{:S(2)}, u32[]{:S(2)}) collective-permute-start(bf16[64,512]{1,0:T(8,128)(2,1)S(1)} %copy-done.7), channel_id=1, source_target_pairs={{0,24},{8,0},{16,8},{24,16},{1,25},{9,1},{17,9},{25,17},{2,26},{10... | collective-permute-start | bytes 196616 | tf_op jit(solution)/shard_map/ppermute | solution.py:31
  140.1 4.6 %collective-permute-done.9.refs_2_ = bf16[64,512]{1,0:T(8,128)(2,1)S(1)} collective-permute-done((bf16[64,512]{1,0:T(8,128)(2,1)S(1)}, bf16[64,512]{1,0:T(8,128)(2,1)S(1)}, u32[]{:S(2)}, u32[]{:S(2)}) %collective-permute-start.9) | collective-permute-done | bytes 65568 | tf_op jit(solution)/shard_map/ppermute | solution.py:31
  145.3 15.3 %all-to-all-done.3.slices_ref = bf16[8,8,8192]{2,1,0:T(8,128)(2,1)S(1)} async-done(((bf16[8,8,8192]{2,1,0:T(8,128)(2,1)}), bf16[8,8,8192]{2,1,0:T(8,128)(2,1)S(1)}, u32[]{:S(2)}, u32[]{:S(2)}) %all-to-all-start.3) | async-done | bytes 1048608 | tf_op jit(solution)/shard_map/all_to_all | solution.py:26
  161.8 3.7 %all-to-all-start.4 = ((bf16[8,8,8192]{2,1,0:T(8,128)(2,1)}), bf16[8,8,8192]{2,1,0:T(8,128)(2,1)S(1)}, u32[]{:S(2)}, u32[]{:S(2)}) async-start(bf16[8,8,8192]{2,1,0:T(8,128)(2,1)} %sums_above.1.refs_0_), calls=%async_computation.4 | async-start | bytes 2097152 | tf_op jit(solution)/shard_map/all_to_all | solution.py:26
  165.5 3.6 %collective-permute-start.11 = (bf16[4,72,256]{2,1,0:T(8,128)(2,1)S(1)}, bf16[4,72,256]{2,1,0:T(8,128)(2,1)S(1)}, u32[]{:S(2)}, u32[]{:S(2)}) collective-permute-start(bf16[4,72,256]{2,1,0:T(8,128)(2,1)S(1)} %get-tuple-element.34), channel_id=1, source_target_pairs={{0,4},{1,5},{2,6},{3,7},{4,0},{5,1},{6,2},{7,3},{8,12},{9,13},{10,... | collective-permute-start | bytes 442376 | tf_op jit(solution)/shard_map/ppermute | solution.py:35
  169.1 9.2 %collective-permute-done.11.refs_1_ = bf16[4,72,256]{2,1,0:T(8,128)(2,1)S(1)} collective-permute-done((bf16[4,72,256]{2,1,0:T(8,128)(2,1)S(1)}, bf16[4,72,256]{2,1,0:T(8,128)(2,1)S(1)}, u32[]{:S(2)}, u32[]{:S(2)}) %collective-permute-start.11) | collective-permute-done | bytes 147488 | tf_op jit(solution)/shard_map/ppermute | solution.py:35
  180.3 6.4 %collective-permute-done.12.refs_1_ = bf16[2,72,256]{2,1,0:T(8,128)(2,1)S(1)} collective-permute-done((bf16[2,72,256]{2,1,0:T(8,128)(2,1)S(1)}, bf16[2,72,256]{2,1,0:T(8,128)(2,1)S(1)}, u32[]{:S(2)}, u32[]{:S(2)}) %collective-permute-start.12) | collective-permute-done | bytes 73760 | tf_op jit(solution)/shard_map/ppermute | solution.py:35
  188.6 3.1 %collective-permute-done.13.refs_1_ = bf16[1,72,256]{2,1,0:T(8,128)(2,1)S(1)} collective-permute-done((bf16[1,72,256]{2,1,0:T(8,128)(2,1)S(1)}, bf16[1,72,256]{2,1,0:T(8,128)(2,1)S(1)}, u32[]{:S(2)}, u32[]{:S(2)}) %collective-permute-start.13) | collective-permute-done | bytes 36896 | tf_op jit(solution)/shard_map/ppermute | solution.py:35
  196.8 5.5 %all_to_all.30 = bf16[2,64,8192]{2,1,0:T(8,128)(2,1)S(1)} all-to-all(bf16[2,64,8192]{2,1,0:T(8,128)(2,1)S(1)} %pad_maximum_fusion), channel_id=1, replica_groups=mesh['y'=8,'core'=2,'x'=4,'z'=8] {'core'}, dimensions={0} | all-to-all | bytes 4194304 | tf_op jit(solution)/shard_map/all_to_all | solution.py:26
  (58 shorter events, 46.7 us)
Async XLA Ops:
  4.2 32.3 %copy-start.5 = (f32[1,8192]{1,0:T(1,128)S(1)}, f32[1,8192]{1,0:T(1,128)}, u32[]{:S(2)}) copy-start(f32[1,8192]{1,0:T(1,128)} %gain_ref.1) | copy-start | bytes 98308
  6.7 32.9 %all-to-all-start = ((bf16[4,128,1024]{2,1,0:T(8,128)(2,1)}), bf16[4,128,1024]{2,1,0:T(8,128)(2,1)S(1)}, u32[]{:S(2)}, u32[]{:S(2)}) async-start(bf16[4,128,1024]{2,1,0:T(8,128)(2,1)} %mask.1), calls=%async_computation | async-start | bytes 2097152 | tf_op jit(solution)/shard_map/all_to_all | solution.py:26
  11.5 23.0 %collective-permute-start.1 = (bf16[272,1024]{1,0:T(8,128)(2,1)}, bf16[272,1024]{1,0:T(8,128)(2,1)}, u32[]{:S(2)}, u32[]{:S(2)}) collective-permute-start(bf16[272,1024]{1,0:T(8,128)(2,1)} %fold.1.refs_0_), channel_id=1, source_target_pairs={{0,1},{1,2},{2,3},{3,4},{4,5},{5,6},{6,7},{7,0},{8,9},{9,10},{10,1... | collective-permute-start | bytes 1671176 | tf_op jit(solution)/shard_map/ppermute | solution.py:31
  15.5 28.0 %collective-permute-start.5 = (bf16[272,1024]{1,0:T(8,128)(2,1)}, bf16[272,1024]{1,0:T(8,128)(2,1)}, u32[]{:S(2)}, u32[]{:S(2)}) collective-permute-start(bf16[272,1024]{1,0:T(8,128)(2,1)} %fold.1.refs_0_), channel_id=1, source_target_pairs={{0,7},{1,0},{2,1},{3,2},{4,3},{5,4},{6,5},{7,6},{8,15},{9,8},{10,9... | collective-permute-start | bytes 1671176 | tf_op jit(solution)/shard_map/ppermute | solution.py:31
  34.5 16.0 %collective-permute-start.2 = (bf16[272,1024]{1,0:T(8,128)(2,1)}, bf16[272,1024]{1,0:T(8,128)(2,1)}, u32[]{:S(2)}, u32[]{:S(2)}) collective-permute-start(bf16[272,1024]{1,0:T(8,128)(2,1)} %collective-permute-done.1.refs_1_), channel_id=1, source_target_pairs={{0,1},{1,2},{2,3},{3,4},{4,5},{5,6},{6,7},{7,0},{8,9},{9,10},{10,1... | collective-permute-start | bytes 1671176 | tf_op jit(solution)/shard_map/ppermute | solution.py:31
  39.6 39.3 %all-to-all-start.1 = ((bf16[4,128,2048]{2,1,0:T(8,128)(2,1)}), bf16[4,128,2048]{2,1,0:T(8,128)(2,1)S(1)}, u32[]{:S(2)}, u32[]{:S(2)}) async-start(bf16[4,128,2048]{2,1,0:T(8,128)(2,1)} %normalise.1), calls=%async_computation.1 | async-start | bytes 4194304 | tf_op jit(solution)/shard_map/all_to_all | solution.py:26
  43.5 14.4 %collective-permute-start.6 = (bf16[272,1024]{1,0:T(8,128)(2,1)}, bf16[272,1024]{1,0:T(8,128)(2,1)}, u32[]{:S(2)}, u32[]{:S(2)}) collective-permute-start(bf16[272,1024]{1,0:T(8,128)(2,1)} %collective-permute-done.5.refs_2_), channel_id=1, source_target_pairs={{0,7},{1,0},{2,1},{3,2},{4,3},{5,4},{6,5},{7,6},{8,15},{9,8},{10,9... | collective-permute-start | bytes 1671176 | tf_op jit(solution)/shard_map/ppermute | solution.py:31
  50.5 15.1 %collective-permute-start.3 = (bf16[272,1024]{1,0:T(8,128)(2,1)}, bf16[272,1024]{1,0:T(8,128)(2,1)}, u32[]{:S(2)}, u32[]{:S(2)}) collective-permute-start(bf16[272,1024]{1,0:T(8,128)(2,1)} %collective-permute-done.2.refs_0_), channel_id=1, source_target_pairs={{0,1},{1,2},{2,3},{3,4},{4,5},{5,6},{6,7},{7,0},{8,9},{9,10},{10,1... | collective-permute-start | bytes 1671176 | tf_op jit(solution)/shard_map/ppermute | solution.py:31
  57.9 21.0 %collective-permute-start.7 = (bf16[272,1024]{1,0:T(8,128)(2,1)}, bf16[272,1024]{1,0:T(8,128)(2,1)}, u32[]{:S(2)}, u32[]{:S(2)}) collective-permute-start(bf16[272,1024]{1,0:T(8,128)(2,1)} %collective-permute-done.6.refs_1_), channel_id=1, source_target_pairs={{0,7},{1,0},{2,1},{3,2},{4,3},{5,4},{6,5},{7,6},{8,15},{9,8},{10,9... | collective-permute-start | bytes 1671176 | tf_op jit(solution)/shard_map/ppermute | solution.py:31
  65.6 16.1 %collective-permute-start.4 = (bf16[272,1024]{1,0:T(8,128)(2,1)}, bf16[272,1024]{1,0:T(8,128)(2,1)}, u32[]{:S(2)}, u32[]{:S(2)}) collective-permute-start(bf16[272,1024]{1,0:T(8,128)(2,1)} %collective-permute-done.3.refs_0_), channel_id=1, source_target_pairs={{0,1},{1,2},{2,3},{3,4},{4,5},{5,6},{6,7},{7,0},{8,9},{9,10},{10,1... | collective-permute-start | bytes 1671176 | tf_op jit(solution)/shard_map/ppermute | solution.py:31
  67.5 29.4 %collective-permute-start = (bf16[128,8192]{1,0:T(8,128)(2,1)}, bf16[128,8192]{1,0:T(8,128)(2,1)}, u32[]{:S(2)}, u32[]{:S(2)}) collective-permute-start(bf16[128,8192]{1,0:T(8,128)(2,1)} %bitcast.25), channel_id=1, source_target_pairs={{0,32},{32,0},{1,33},{33,1},{2,34},{34,2},{3,35},{35,3},{4,36},{36... | collective-permute-start | bytes 6291464 | tf_op jit(solution)/shard_map/ppermute | solution.py:35
  84.6 8.8 %copy-start.1 = (bf16[1,64,1024]{2,1,0:T(8,128)(2,1)S(1)}, bf16[1,64,1024]{2,1,0:T(8,128)(2,1)}, u32[]{:S(2)}) copy-start(bf16[1,64,1024]{2,1,0:T(8,128)(2,1)} %param.12) | copy-start | bytes 393220
  84.6 33.1 %all-to-all-start.2 = ((bf16[8,64,2048]{2,1,0:T(8,128)(2,1)}), bf16[8,64,2048]{2,1,0:T(8,128)(2,1)}, u32[]{:S(2)}, u32[]{:S(2)}) async-start(bf16[8,64,2048]{2,1,0:T(8,128)(2,1)} %get-tuple-element.27.refs_0_), calls=%async_computation.2 | async-start | bytes 4194304 | tf_op jit(solution)/shard_map/all_to_all | solution.py:26
  93.4 1.0 copy-start.4
  124.4 7.0 %copy-start.7 = (bf16[64,512]{1,0:T(8,128)(2,1)S(1)}, bf16[64,512]{1,0:T(8,128)(2,1)}, u32[]{:S(2)}) copy-start(bf16[64,512]{1,0:T(8,128)(2,1)} %copy-done.6) | copy-start | bytes 196612
  124.4 36.2 %all-to-all-start.3 = ((bf16[8,8,8192]{2,1,0:T(8,128)(2,1)}), bf16[8,8,8192]{2,1,0:T(8,128)(2,1)S(1)}, u32[]{:S(2)}, u32[]{:S(2)}) async-start(bf16[8,8,8192]{2,1,0:T(8,128)(2,1)} %bitcast.28), calls=%async_computation.3 | async-start | bytes 2097152 | tf_op jit(solution)/shard_map/all_to_all | solution.py:26
  131.4 8.7 %collective-permute-start.10 = (bf16[64,512]{1,0:T(8,128)(2,1)S(1)}, bf16[64,512]{1,0:T(8,128)(2,1)S(1)}, u32[]{:S(2)}, u32[]{:S(2)}) collective-permute-start(bf16[64,512]{1,0:T(8,128)(2,1)S(1)} %copy-done.7), channel_id=1, source_target_pairs={{0,16},{8,24},{16,0},{24,8},{1,17},{9,25},{17,1},{25,9},{2,18},{10... | collective-permute-start | bytes 196616 | tf_op jit(solution)/shard_map/ppermute | solution.py:31
  133.9 6.2 %collective-permute-start.8 = (bf16[64,512]{1,0:T(8,128)(2,1)S(1)}, bf16[64,512]{1,0:T(8,128)(2,1)S(1)}, u32[]{:S(2)}, u32[]{:S(2)}) collective-permute-start(bf16[64,512]{1,0:T(8,128)(2,1)S(1)} %copy-done.7), channel_id=1, source_target_pairs={{0,24},{8,0},{16,8},{24,16},{1,25},{9,1},{17,9},{25,17},{2,26},{10... | collective-permute-start | bytes 196616 | tf_op jit(solution)/shard_map/ppermute | solution.py:31
  138.2 6.5 %collective-permute-start.9 = (bf16[64,512]{1,0:T(8,128)(2,1)S(1)}, bf16[64,512]{1,0:T(8,128)(2,1)S(1)}, u32[]{:S(2)}, u32[]{:S(2)}) collective-permute-start(bf16[64,512]{1,0:T(8,128)(2,1)S(1)} %copy-done.7), channel_id=1, source_target_pairs={{0,8},{8,16},{16,24},{24,0},{1,9},{9,17},{17,25},{25,1},{2,10},{10... | collective-permute-start | bytes 196616 | tf_op jit(solution)/shard_map/ppermute | solution.py:31
  161.8 3.7 %copy-start = (bf16[8,8,8192]{2,1,0:T(8,128)(2,1)S(1)}, bf16[8,8,8192]{2,1,0:T(8,128)(2,1)}, u32[]{:S(2)}) copy-start(bf16[8,8,8192]{2,1,0:T(8,128)(2,1)} %sums_above.1.refs_0_) | copy-start | bytes 3145732
  161.8 32.9 %all-to-all-start.4 = ((bf16[8,8,8192]{2,1,0:T(8,128)(2,1)}), bf16[8,8,8192]{2,1,0:T(8,128)(2,1)S(1)}, u32[]{:S(2)}, u32[]{:S(2)}) async-start(bf16[8,8,8192]{2,1,0:T(8,128)(2,1)} %sums_above.1.refs_0_), calls=%async_computation.4 | async-start | bytes 2097152 | tf_op jit(solution)/shard_map/all_to_all | solution.py:26
  165.5 12.8 %collective-permute-start.11 = (bf16[4,72,256]{2,1,0:T(8,128)(2,1)S(1)}, bf16[4,72,256]{2,1,0:T(8,128)(2,1)S(1)}, u32[]{:S(2)}, u32[]{:S(2)}) collective-permute-start(bf16[4,72,256]{2,1,0:T(8,128)(2,1)S(1)} %get-tuple-element.34), channel_id=1, source_target_pairs={{0,4},{1,5},{2,6},{3,7},{4,0},{5,1},{6,2},{7,3},{8,12},{9,13},{10,... | collective-permute-start | bytes 442376 | tf_op jit(solution)/shard_map/ppermute | solution.py:35
  178.4 8.3 %collective-permute-start.12 = (bf16[2,72,256]{2,1,0:T(8,128)(2,1)S(1)}, bf16[2,72,256]{2,1,0:T(8,128)(2,1)S(1)}, u32[]{:S(2)}, u32[]{:S(2)}) collective-permute-start(bf16[2,72,256]{2,1,0:T(8,128)(2,1)S(1)} %get-tuple-element.36), channel_id=1, source_target_pairs={{0,2},{1,3},{2,0},{3,1},{4,6},{5,7},{6,4},{7,5},{8,10},{9,11},{10,... | collective-permute-start | bytes 221192 | tf_op jit(solution)/shard_map/ppermute | solution.py:35
  186.7 5.0 %collective-permute-start.13 = (bf16[1,72,256]{2,1,0:T(8,128)(2,1)S(1)}, bf16[1,72,256]{2,1,0:T(8,128)(2,1)S(1)}, u32[]{:S(2)}, u32[]{:S(2)}) collective-permute-start(bf16[1,72,256]{2,1,0:T(8,128)(2,1)S(1)} %get-tuple-element.38), channel_id=1, source_target_pairs={{0,1},{1,0},{2,3},{3,2},{4,5},{5,4},{6,7},{7,6},{8,9},{9,8},{10,11... | collective-permute-start | bytes 110600 | tf_op jit(solution)/shard_map/ppermute | solution.py:35
  (3 other events, 2.2 us)

commit v3 on v2

--- a/solution.py
+++ b/solution.py
@@ -15,6 +15,7 @@
 BF16 = jnp.bfloat16
 SMEM = pl.BlockSpec(memory_space=pltpu.SMEM)
 ANY = pl.BlockSpec(memory_space=pl.ANY)
+VMEM = pl.BlockSpec(memory_space=pltpu.VMEM)
 HBM = pl.BlockSpec(memory_space=pltpu.HBM)
 
 
@@ -51,168 +52,199 @@
     return pl.BlockSpec(shape, lambda *_: (0,) * len(shape))
 
 
-def fold_kernel(weight_ref, a_ref, b_ref, out_ref):
+def prepare_kernel(keep_ref, count_ref, weight_ref, a_ref, b_ref, grad_ref, block_ref, masked_ref):
+    grad = grad_ref[...]
+    positions = lax.broadcasted_iota(jnp.int32, (grad.shape[0], 1), 0)
+    live = (positions < count_ref[...]) & (keep_ref[...] > 0)
+    masked = jnp.where(live, grad, jnp.zeros_like(grad))
+    for copy in range(masked_ref.shape[0]):
+        masked_ref[copy] = masked
     rows = weight_ref.shape[0]
     rank, share = a_ref.shape
     low = contract(a_ref[...], b_ref[...], (0, 0))
-    out_ref[:rows] = (weight_ref[...].astype(F32) + ADAPTER_SCALING * low).astype(BF16)
-    groups = out_ref.shape[1] // share
+    block_ref[:rows] = (weight_ref[...].astype(F32) + ADAPTER_SCALING * low).astype(BF16)
+    groups = block_ref.shape[1] // share
     depth = rank // groups
     for group in range(groups):
-        out_ref[rows:, group * share : (group + 1) * share] = a_ref[group * depth : (group + 1) * depth]
-
-
-def fold(weight, a_cols, b_mat):
+        block_ref[rows:, group * share : (group + 1) * share] = a_ref[group * depth : (group + 1) * depth]
+
+
+def prepare(keep, count, weight, a_cols, b_mat, grad, copies):
     rows, key_width = weight.shape
-    packed = a_cols.size // key_width
-    return pl.pallas_call(
-        fold_kernel,
-        grid=(1,),
-        out_shape=jax.ShapeDtypeStruct((rows + packed, key_width), BF16),
-        in_specs=[whole(*weight.shape), whole(*a_cols.shape), whole(*b_mat.shape)],
-        out_specs=whole(rows + packed, key_width),
-        compiler_params=params(),
-        cost_estimate=cost(2 * a_cols.shape[0] * weight.size, 3 * weight.size),
-        name="fold",
-    )(weight, a_cols, b_mat)
-
-
-def mask_kernel(keep_ref, count_ref, grad_ref, *refs):
-    out_ref = refs[-1]
-    grad = grad_ref[...]
-    positions = lax.broadcasted_iota(jnp.int32, (grad.shape[0], 1), 0)
-    limit = jnp.where(keep_ref[0] > 0, count_ref[0], 0)
-    out_ref[0] = jnp.where(positions < limit, grad, jnp.zeros_like(grad))
-
-
-def mask(keep, count, grad, after, copies):
-    return pl.pallas_call(
-        mask_kernel,
-        grid=(copies,),
-        out_shape=pltpu.HBM((copies,) + grad.shape, BF16),
-        in_specs=[SMEM, SMEM, whole(*grad.shape)] + [ANY] * len(after),
-        out_specs=pl.BlockSpec((1,) + grad.shape, lambda i: (i, 0, 0)),
-        compiler_params=params(),
-        cost_estimate=cost(grad.size, 5 * grad.size),
-        name="mask",
-    )(keep, count, grad, *after)
-
-
-def products_kernel(share, count, given, masked_ref, *refs):
+    shapes = ((rows + a_cols.size // key_width, key_width), (copies,) + grad.shape)
+    return pl.pallas_call(
+        prepare_kernel,
+        grid=(1,),
+        out_shape=(jax.ShapeDtypeStruct(shapes[0], BF16), pltpu.HBM(shapes[1], BF16)),
+        in_specs=[whole(*operand.shape) for operand in (keep, count, weight, a_cols, b_mat, grad)],
+        out_specs=tuple(whole(*shape) for shape in shapes),
+        compiler_params=params(),
+        cost_estimate=cost(2 * a_cols.shape[0] * weight.size, 8 * weight.size),
+        name="prepare",
+    )(keep, count, weight, a_cols, b_mat, grad)
+
+
+def products_kernel(share, count, masked_ref, *refs):
     blocks, (out_ref, a_ref) = refs[:count], refs[-2:]
     nx, tokens, key_width = masked_ref.shape
     half = out_ref.shape[1]
     rows = masked_ref[...].reshape(nx * tokens, key_width)
-    at = 0
-    for block in blocks:
-        depth = min(block.shape[0], share)
-        columns = contract(rows, block[:depth], (1, 1)).astype(BF16)
+    for at, block in enumerate(blocks):
+        columns = contract(rows, block[:share], (1, 1)).astype(BF16)
         for chip in range(nx):
             for part in range(tokens // half):
                 start = chip * tokens + part * half
-                out_ref[part * nx + chip, :, at : at + depth] = columns[start : start + half]
-        at += depth
-    slot = 0
-    for ref in refs[count : count + given]:
-        a_ref[slot : slot + ref.shape[0]] = ref[...]
-        slot += ref.shape[0]
-    for block in blocks:
-        if block.shape[0] > share:
-            a_ref[slot] = block[share:]
-            slot += 1
-
-
-def products(masked_x, blocks, share, cores, width, a_parts=(), column=0, into=None, after=()):
+                out_ref[part * nx + chip, :, at * share : (at + 1) * share] = columns[start : start + half]
+    for slot, block in enumerate(blocks):
+        a_ref[slot] = block[share:]
+
+
+def products(masked_x, blocks, share, cores, width, column=0, into=None, after=()):
     nx, tokens, key_width = masked_x.shape
-    columns = sum(min(block.shape[0], share) for block in blocks)
+    columns = share * len(blocks)
     shape = (cores * nx, tokens // cores, width)
     extra = list(after) + ([] if into is None else [into])
-    slots = sum(part.shape[0] for part in a_parts) + sum(block.shape[0] > share for block in blocks)
-    rows = max(block.shape[0] for block in blocks) - share
-    return pl.pallas_call(
-        functools.partial(products_kernel, share, len(blocks), len(a_parts)),
-        grid=(1,),
-        out_shape=(pltpu.HBM(shape, BF16), jax.ShapeDtypeStruct((slots, rows, key_width), BF16)),
+    a_shape = (len(blocks), blocks[0].shape[0] - share, key_width)
+    return pl.pallas_call(
+        functools.partial(products_kernel, share, len(blocks)),
+        grid=(1,),
+        out_shape=(pltpu.HBM(shape, BF16), pltpu.HBM(a_shape, BF16)),
         in_specs=[whole(*masked_x.shape)]
-        + [whole(*value.shape) for value in (*blocks, *a_parts)]
+        + [whole(*value.shape) for value in blocks]
         + [ANY] * len(after)
         + [HBM] * (into is not None),
         out_specs=(
             pl.BlockSpec(shape[:2] + (columns,), lambda i: (0, 0, column // columns)),
-            whole(slots, rows, key_width),
+            whole(*a_shape),
         ),
-        input_output_aliases={} if into is None else {len(blocks) + len(a_parts) + len(extra): 0},
+        input_output_aliases={} if into is None else {len(blocks) + len(extra): 0},
         compiler_params=params(20),
         cost_estimate=cost(2 * masked_x.size * columns, 2 * masked_x.size),
         name="products",
-    )(masked_x, *blocks, *a_parts, *extra)
-
-
-def term_kernel(share, offsets, nz, place_ref, own_ref, other_ref, gain_ref, *refs):
-    pieces, (term_ref, total_ref) = refs[: len(offsets)], refs[-2:]
+    )(masked_x, *blocks, *extra)
+
+
+def inverse_kernel(share, rows, core_ref, own_ref, other_ref, *refs):
+    out_ref = refs[-1]
+    half = out_ref.shape[1]
+    width = own_ref.shape[1]
+    for slot, hidden_ref in enumerate((own_ref, other_ref)):
+        for at in range(0, half, rows):
+            span = pl.ds(pl.multiple_of(core_ref[0] * half + at, rows), rows)
+            squares = jnp.zeros((rows, share), F32)
+            for column in range(0, width, share):
+                hidden = hidden_ref[span, column : column + share].astype(F32)
+                squares += hidden * hidden
+            inv = lax.rsqrt(jnp.sum(squares, axis=1, keepdims=True) * (1.0 / width) + EPS)
+            out_ref[slot, at : at + rows] = jnp.broadcast_to(inv, (rows, out_ref.shape[2]))
+
+
+def inverses(core, hidden, other, after, share):
+    shape = (2, hidden.shape[0] // 2, 128)
+    return pl.pallas_call(
+        functools.partial(inverse_kernel, share, 32),
+        grid=(1,),
+        out_shape=jax.ShapeDtypeStruct(shape, F32),
+        in_specs=[SMEM, whole(*hidden.shape), whole(*other.shape)] + [HBM] * len(after),
+        out_specs=whole(*shape),
+        compiler_params=params(16),
+        cost_estimate=cost(3 * hidden.size, 2 * hidden.size),
+        name="inverses",
+    )(core, hidden, other, *after)
+
+
+def term_kernel(share, offsets, place_ref, own_ref, other_ref, inv_ref, gain_ref, piece_ref, *refs):
+    mine_ref, theirs_ref, total_ref = refs[-3:]
     rows, width = own_ref.shape
-    nx = pieces[0].shape[0] // 2
+    nz = len(offsets)
+    nx = piece_ref.shape[0] // 2
     z, core = place_ref[0], place_ref[1]
-
-    def places():
-        for chip in range(nx):
-            for piece, piece_offsets in zip(pieces, offsets):
-                for at, offset in enumerate(piece_offsets):
-                    slot = lax.rem(z + (offset + nz), nz)
-                    start = pl.multiple_of(chip * (nz * share) + slot * share, share)
-                    yield chip, piece, slice(at * share, (at + 1) * share), pl.ds(start, share)
+    columns = []
+    for chip in range(nx):
+        for at, offset in enumerate(offsets):
+            slot = lax.rem(z + (offset + nz), nz)
+            start = pl.multiple_of(chip * (nz * share) + slot * share, share)
+            columns.append((chip, slice(at * share, (at + 1) * share), pl.ds(start, share)))
 
     layers = ((own_ref, core), (other_ref, 1 - core))
     factors = []
-    for hidden_ref, layer in layers:
+    for index, (hidden_ref, layer) in enumerate(layers):
         partial = jnp.zeros((rows, share), F32)
-        squares = jnp.zeros((rows, share), F32)
-        for chip, piece, cols, place in places():
-            slope = gain_ref[layer, :, place] * piece[layer * nx + chip, :, cols].astype(F32)
-            hidden = hidden_ref[:, place].astype(F32)
-            partial += hidden * slope
-            squares += hidden * hidden
-        inv = lax.rsqrt(jnp.sum(squares, axis=1, keepdims=True) * (1.0 / width) + EPS)
+        for chip, cols, place in columns:
+            slope = gain_ref[layer, :, place] * piece_ref[layer * nx + chip, :, cols].astype(F32)
+            partial += hidden_ref[:, place].astype(F32) * slope
+        inv = inv_ref[index, :, :1]
         inner = jnp.sum(partial, axis=1, keepdims=True) * (1.0 / width)
         factors.append((inv, inv * inv * inner))
-    for chip, piece, cols, place in places():
-        total = None
+    for chip, cols, place in columns:
+        terms = []
         for (hidden_ref, layer), (inv, factor) in zip(layers, factors):
-            slope = gain_ref[layer, :, place] * piece[layer * nx + chip, :, cols].astype(F32)
-            term = (inv * (slope - hidden_ref[:, place].astype(F32) * factor)).astype(BF16)
-            term_ref[layer, :, place] = term
-            total = term.astype(F32) if total is None else total + term.astype(F32)
-        total_ref[:, place] = total.astype(BF16)
-
-
-def norm_backward(place, hidden, other, gain_pair, pieces, offsets, after, share, nz):
+            slope = gain_ref[layer, :, place] * piece_ref[layer * nx + chip, :, cols].astype(F32)
+            terms.append((inv * (slope - hidden_ref[:, place].astype(F32) * factor)).astype(BF16))
+        total = (terms[0].astype(F32) + terms[1].astype(F32)).astype(BF16)
+        total_ref[:, place] = total
+        mine_ref[:, place] = jnp.where(core > 0, terms[0], total)
+        theirs_ref[:, place] = jnp.where(core > 0, total, terms[1])
+
+
+def norm_backward(place, hidden, other, inv_pair, gain_pair, piece, offsets, after, share):
     half, width = other.shape[0] // 2, other.shape[1]
     rows = 16
     steps = half // rows
+    half_block = pl.BlockSpec((rows, width), lambda i, at: (at[1] * steps + i, 0))
+    row_block = pl.BlockSpec((rows, width), lambda i, at: (i, 0))
 
     def by_rows(array):
         return pl.BlockSpec((array.shape[0], rows, array.shape[2]), lambda i, at: (0, i, 0))
 
-    half_block = pl.BlockSpec((rows, width), lambda i, at: (at[1] * steps + i, 0))
-    return pl.pallas_call(
-        functools.partial(term_kernel, share, offsets, nz),
+    return pl.pallas_call(
+        functools.partial(term_kernel, share, offsets),
         grid_spec=pltpu.PrefetchScalarGridSpec(
             num_scalar_prefetch=1,
             grid=(steps,),
-            in_specs=[
-                half_block,
-                half_block,
-                whole(*gain_pair.shape),
-            ]
-            + [by_rows(piece) for piece in pieces]
+            in_specs=[half_block, half_block, by_rows(inv_pair), whole(*gain_pair.shape), by_rows(piece)]
             + [ANY] * len(after),
-            out_specs=(pl.BlockSpec((2, rows, width), lambda i, at: (0, i, 0)), pl.BlockSpec((rows, width), lambda i, at: (i, 0))),
+            out_specs=(row_block,) * 3,
         ),
-        out_shape=(pltpu.HBM((2, half, width), BF16), pltpu.HBM((half, width), BF16)),
-        compiler_params=params(),
+        out_shape=(pltpu.HBM((half, width), BF16),) * 3,
+        compiler_params=params(16),
         cost_estimate=cost(20 * hidden.size, 4 * hidden.size),
         name="norm_backward",
-    )(place, hidden, other, gain_pair, *pieces, *after)
+    )(place, hidden, other, inv_pair, gain_pair, piece, *after)
+
+
+def stream_kernel(core_ref, above_ref, sum_ref, *refs):
+    refs[-1][...] = (above_ref[...].astype(F32) + sum_ref[...].astype(F32)).astype(BF16)
+
+
+def stream_rows_kernel(core_ref, above_ref, sum_ref, whole_ref, out_ref):
+    rows = out_ref.shape[0]
+    span = pl.ds(pl.multiple_of(pl.program_id(0) * rows, rows), rows)
+    out_ref[...] = (above_ref[span].astype(F32) + sum_ref[span].astype(F32)).astype(BF16)
+
+
+def stream_half(core, above, within, into=None):
+    half, width = above.shape
+    rows = 16
+    steps = half // rows
+    own = into is None
+    sources = [pl.BlockSpec((rows, width), lambda i, at: (i, 0)) if own else pl.BlockSpec(memory_space=pltpu.VMEM)] * 2
+    return pl.pallas_call(
+        stream_kernel if own else stream_rows_kernel,
+        grid_spec=pltpu.PrefetchScalarGridSpec(
+            num_scalar_prefetch=1,
+            grid=(steps,),
+            in_specs=sources + ([] if own else [HBM]),
+            out_specs=pl.BlockSpec(
+                (rows, width), lambda i, at: ((at[0] if own else 1 - at[0]) * steps + i, 0)
+            ),
+        ),
+        out_shape=pltpu.HBM((2 * half, width), BF16),
+        input_output_aliases={} if own else {3: 0},
+        compiler_params=params(),
+        cost_estimate=cost(above.size, 3 * above.size),
+        name="stream_half",
+    )(core, above, within, *([] if own else [into]))
 
 
 def above_kernel(slices_ref, *refs):
@@ -269,7 +301,7 @@
     )(hidden, gain)
 
 
-def partials_kernel(share, offsets, nz, scale_factor, z_ref, masked_ref, normed_ref, a_ref, b_ref, *refs):
+def partials_kernel(share, offsets, nz, scale_factor, z_ref, masked_ref, normed_ref, b_ref, *refs):
     part_ref, projected_ref = refs[-2:]
     nx, tokens, key_width = masked_ref.shape
     lowrank = contract(masked_ref[...].reshape(nx * tokens, key_width), b_ref[...], (1, 1)).astype(BF16)
@@ -277,20 +309,21 @@
         normed = normed_ref[:, :, at * share : (at + 1) * share].reshape(nx * tokens, share)
         part_ref[at] = (scale_factor * contract(lowrank, normed, (0, 0))).astype(BF16)
     total = jnp.zeros(projected_ref.shape, F32)
-    for at, offset in enumerate(offsets):
-        slot = lax.rem(z_ref[0] + (offset + nz), nz)
-        place = pl.ds(pl.multiple_of(slot * share, share), share)
-        packed = a_ref[at]
-        groups = packed.shape[1] // share
-        a_cols = jnp.concatenate([packed[:, g * share : (g + 1) * share] for g in range(groups)], axis=0)
-        total += contract(a_cols, normed_ref[:, :, place].reshape(nx * tokens, share), (1, 1))
+    for ref, ref_offsets in zip(refs, offsets):
+        for at, offset in enumerate(ref_offsets):
+            slot = lax.rem(z_ref[0] + (offset + nz), nz)
+            place = pl.ds(pl.multiple_of(slot * share, share), share)
+            packed = ref[at]
+            groups = packed.shape[1] // share
+            a_cols = jnp.concatenate([packed[:, g * share : (g + 1) * share] for g in range(groups)], axis=0)
+            total += contract(a_cols, normed_ref[:, :, place].reshape(nx * tokens, share), (1, 1))
     projected_ref[...] = total.astype(BF16)
 
 
-def partials(z, masked_x, normed_x, a_own, b_mat, offsets, after, share, nz, scale_factor):
+def partials(z, masked_x, normed_x, b_mat, a_rows, offsets, after, share, nz, scale_factor):
     nx, tokens, _ = masked_x.shape
     rank = b_mat.shape[0]
-    operands = (masked_x, normed_x, a_own, b_mat)
+    operands = (masked_x, normed_x, b_mat, *a_rows)
     shapes = ((nz, rank, share), (rank, nx * tokens))
     return pl.pallas_call(
         functools.partial(partials_kernel, share, offsets, nz, scale_factor),
@@ -385,10 +418,16 @@
     )(side, *values)
 
 
-def scatter_sum(part_a, part_b, axis, after=()):
+def scatter_begin(part_a, part_b, axis):
     bit = lax.axis_size(axis) // 2
     index = lax.axis_index(axis)
-    kept, sent = halves(part_a, part_b, ((index // bit) % 2)[None], after)
+    kept, sent = halves(part_a, part_b, ((index // bit) % 2)[None], [])
+    return add([kept, swap(sent, axis, bit)], ((index // (bit // 2)) % 2)[None])
+
+
+def scatter_end(kept, sent, axis):
+    bit = lax.axis_size(axis) // 4
+    index = lax.axis_index(axis)
     while bit > 1:
         received = swap(sent, axis, bit)
         bit //= 2
@@ -408,8 +447,10 @@
     scale_factor = ADAPTER_SCALING / math.sqrt(tokens * replicas)
     x_index, z_index, core = (lax.axis_index(axis) for axis in ("x", "z", "core"))
 
-    block = fold(in_hbm(key_weight[0]), in_hbm(adapter_a[0]), in_hbm(adapter_b[0]))
-    masked = mask(keep_flags, valid_counts, in_hbm(key_grad[0]), [block], nx)
+    b_mat = in_hbm(adapter_b[0])
+    block, masked = prepare(
+        keep_flags[None], valid_counts[None], in_hbm(key_weight[0]), in_hbm(adapter_a[0]), b_mat, in_hbm(key_grad[0]), nx
+    )
     masked_x = exchange(masked, "x")
     up, down = [block], [block]
     for step in range(1, nz // 2):
@@ -418,7 +459,7 @@
     up.append(shift(up[-1], "z", 1))
 
     hidden = in_hbm(hidden_in[0])
-    other = in_hbm(swap(hidden, "core", 1))
+    other = swap(hidden, "core", 1)
     gain_pair = lax.all_gather(norm_gain, "core", axis=0, tiled=True)[:, None, :]
 
     rounds = [
@@ -428,41 +469,44 @@
         ([up[4]], [-4], 3),
     ]
     normed_x = exchange(normalise(hidden, norm_gain, share, nx), "x")
-    dnorm, a_own = None, None
+    dnorm, a_rows = None, []
     for blocks, _, slot in rounds:
-        dnorm, a_own = products(
+        dnorm, rows = products(
             masked_x,
             blocks,
             share,
             cores,
             nz * share,
-            [] if a_own is None else [a_own],
             column=slot * share,
             into=dnorm,
             after=[normed_x] if slot == 6 else [],
         )
-    a_offsets = [offset for _, round_offsets, _ in rounds for offset in round_offsets]
+        a_rows.append(rows)
+    a_offsets = [round_offsets for _, round_offsets, _ in rounds]
     offsets = [0, -1, 1, -4, -2, 2, -3, 3]
     dnorm = in_hbm(dnorm)
-    piece = in_hbm(exchange(dnorm, ("core", "x")))
+    piece = exchange(dnorm, ("core", "x"))
 
     part_a, projected = partials(
-        z_index[None], masked_x, normed_x, a_own, adapter_b[0], a_offsets, [dnorm], share, nz, scale_factor
+        z_index[None], masked_x, normed_x, b_mat, a_rows, a_offsets, [dnorm], share, nz, scale_factor
     )
     projected = [projected] + [shift(projected, "x", by) for by in (-1, 1, 2)]
     part_b = partial_b(x_index[None], masked_x, projected, scale_factor)
     part_b = part_b.reshape(rank, nz, key_width // replicas).transpose(1, 0, 2).reshape(nz, -1, share)
-    term, total = norm_backward(
-        jnp.stack([z_index, core]), hidden, other, gain_pair, [piece], [offsets], [part_a], share, nz
+    inv_pair = inverses(core[None], hidden, other, [dnorm], share)
+    mine, theirs, total = norm_backward(
+        jnp.stack([z_index, core]), hidden, other, inv_pair, gain_pair, piece, offsets, [part_a], share
     )
 
     slices = exchange(total.reshape(chips_y, half // chips_y, width), "y")
-    above_slices = sums_above(slices, [part_b])
-    above = exchange(above_slices, "y").reshape(half, width).astype(F32)
-    stream_upper = (above + term[1].astype(F32)).astype(BF16)
-    stream_lower = (stream_upper.astype(F32) + term[0].astype(F32)).astype(BF16)
-    stream = exchange(jnp.stack([stream_lower, stream_upper]), "core").reshape(tokens, width)
-    summed = scatter_sum(part_a, part_b, "z", [above_slices])
+    kept, sent = scatter_begin(part_a, part_b, "z")
+    above_slices = sums_above(slices, [kept])
+    beyond = swap(theirs, "core", 1)
+    above = exchange(above_slices, "y").reshape(half, width)
+    summed = scatter_end(kept, sent, "z")
+    above, summed = lax.optimization_barrier((above, summed))
+    received = swap(above, "core", 1)
+    stream = stream_half(core[None], received, beyond, stream_half(core[None], above, mine))
     grad_a = summed[:rank]
     grad_b = summed[rank:].reshape(rank, key_width // replicas)
     return stream[None], grad_a[None], grad_b[None]

time: 205 us -> 201 us (0.980)
  starting transfers between devices: 75.8 us -> 83.5 us
  waiting for transfers between devices: 81.5 us -> 74.9 us
  Pallas kernels: 28.2 us -> 34.3 us
  blocking collectives: 7.51 us -> 1.84 us
  local copies, waits for them, and re-layouts: 6.22 us -> 2.42 us
  other arithmetic: 2.25 us -> 0.07 us
    ppermute x4 -> x6, starting transfers between devices: 12.7 us -> 20.8 us  [swap(): lax.ppermute(value, axis, [(i, i ^ bit) for i in range(lax.axis_size(axis...]
    all_to_all x1 -> x0, blocking collectives: 5.53 us -> none  [exchange(): return lax.all_to_all(value, axes, 0, 0, tiled=True)]
    pallas_call x7 -> x9, Pallas kernels: 21.7 us -> 27 us  [the longest x4 11.2 us: products(): pl.pallas_call(functools.partial(products_kernel, share, len(blocks)), gr...]
    all_to_all x5, waiting for transfers between devices: 37.6 us -> 33.8 us  [exchange(): return lax.all_to_all(value, axes, 0, 0, tiled=True)]
    unnamed x18 -> x17, local copies, waits for them, and re-layouts: 5.14 us -> 1.34 us
    ppermute x4 -> x6, waiting for transfers between devices: 18.6 us -> 15.8 us  [swap(): lax.ppermute(value, axis, [(i, i ^ bit) for i in range(lax.axis_size(axis...]
  transfers between devices with their start and end apart: 19 -> 21, of which waited for: 11 -> 11; matrix products, arithmetic and copies ran while one was open for 1% -> 1% of each run, Pallas kernels for 8% -> 11%
where the time goes in v3:
time: 201 us; the launch traced here: 199 us
  starting transfers between devices  83.5 us (42%)
  waiting for transfers between devices  74.9 us (37%)
  Pallas kernels  34.3 us (17%)
  local copies, waits for them, and re-layouts  2.42 us (1%)
  between operations  2.3 us (1%)
    ppermute x10, starting transfers between devices, shift(): lax.ppermute(value, axis, [(i, (i + by) % size) for i in range(size)])  36.9 us
    all_to_all x5, waiting for transfers between devices, exchange(): return lax.all_to_all(value, axes, 0, 0, tiled=True)  33.8 us
    all_to_all x5, starting transfers between devices, exchange(): return lax.all_to_all(value, axes, 0, 0, tiled=True)  25.8 us
    ppermute x10, waiting for transfers between devices, shift(): lax.ppermute(value, axis, [(i, (i + by) % size) for i in range(size)])  25.3 us
    ppermute x6, starting transfers between devices, swap(): lax.ppermute(value, axis, [(i, i ^ bit) for i in range(lax.axis_size(axis...  20.8 us
    ppermute x6, waiting for transfers between devices, swap(): lax.ppermute(value, axis, [(i, i ^ bit) for i in range(lax.axis_size(axis...  15.8 us
    pallas_call x4, Pallas kernels, products(): pl.pallas_call(functools.partial(products_kernel, share, len(blocks)), gr...  11.2 us
    pallas_call x1, Pallas kernels, norm_backward(): pl.pallas_call(functools.partial(term_kernel, share, offsets), grid_spec=...  6.21 us
  transfers between devices with their start and end apart: 21, of which 11 were waited for; matrix products, arithmetic and copies ran while one was open for 1% of the time, Pallas kernels for 11%

profile of v3, /device:TPU:1, one launch (start us, length us, event | category | flops | bytes accessed | tf_op | source)
XLA Modules:
  0.0 199.2 jit_solution(17905662377718923816)
XLA Ops:
  4.6 4.8 %all-to-all-start = ((bf16[4,128,1024]{2,1,0:T(8,128)(2,1)}), bf16[4,128,1024]{2,1,0:T(8,128)(2,1)S(1)}, u32[]{:S(2)}, u32[]{:S(2)}) async-start(bf16[4,128,1024]{2,1,0:T(8,128)(2,1)} %get-tuple-element.26), calls=%async_computation | async-start | bytes 2097152 | tf_op jit(solution)/shard_map/all_to_all | solution.py:27
  9.4 4.0 %collective-permute-start.1 = (bf16[272,1024]{1,0:T(8,128)(2,1)}, bf16[272,1024]{1,0:T(8,128)(2,1)}, u32[]{:S(2)}, u32[]{:S(2)}) collective-permute-start(bf16[272,1024]{1,0:T(8,128)(2,1)} %get-tuple-element.27.refs_0_), channel_id=1, source_target_pairs={{0,1},{1,2},{2,3},{3,4},{4,5},{5,6},{6,7},{7,0},{8,9},{9,10},{10,1... | collective-permute-start | bytes 1671176 | tf_op jit(solution)/shard_map/ppermute | solution.py:32
  13.4 8.6 %collective-permute-start.5 = (bf16[272,1024]{1,0:T(8,128)(2,1)}, bf16[272,1024]{1,0:T(8,128)(2,1)}, u32[]{:S(2)}, u32[]{:S(2)}) collective-permute-start(bf16[272,1024]{1,0:T(8,128)(2,1)} %get-tuple-element.27.refs_0_), channel_id=1, source_target_pairs={{0,7},{1,0},{2,1},{3,2},{4,3},{5,4},{6,5},{7,6},{8,15},{9,8},{10,9... | collective-permute-start | bytes 1671176 | tf_op jit(solution)/shard_map/ppermute | solution.py:32
  22.0 10.4 %collective-permute-done.1.refs_1_ = bf16[272,1024]{1,0:T(8,128)(2,1)} collective-permute-done((bf16[272,1024]{1,0:T(8,128)(2,1)}, bf16[272,1024]{1,0:T(8,128)(2,1)}, u32[]{:S(2)}, u32[]{:S(2)}) %collective-permute-start.1) | collective-permute-done | bytes 557088 | tf_op jit(solution)/shard_map/ppermute | solution.py:32
  34.4 3.1 %normalise.1 = bf16[4,128,2048]{2,1,0:T(8,128)(2,1)} custom-call(bf16[128,8192]{1,0:T(8,128)(2,1)} %bitcast.30, f32[1,8192]{1,0:T(1,128)S(1)} %copy-done.1), custom_call_target="tpu_custom_call" | custom-call | flops 6291456 | bytes 4194304 | tf_op jit(solution)/shard_map/normalise/pallas_call | solution.py:292
  37.4 3.9 %all-to-all-start.1 = ((bf16[4,128,2048]{2,1,0:T(8,128)(2,1)}), bf16[4,128,2048]{2,1,0:T(8,128)(2,1)S(1)}, u32[]{:S(2)}, u32[]{:S(2)}) async-start(bf16[4,128,2048]{2,1,0:T(8,128)(2,1)} %normalise.1), calls=%async_computation.1 | async-start | bytes 4194304 | tf_op jit(solution)/shard_map/all_to_all | solution.py:27
  41.4 4.6 %collective-permute-start.6 = (bf16[272,1024]{1,0:T(8,128)(2,1)}, bf16[272,1024]{1,0:T(8,128)(2,1)}, u32[]{:S(2)}, u32[]{:S(2)}) collective-permute-start(bf16[272,1024]{1,0:T(8,128)(2,1)} %collective-permute-done.5.refs_2_), channel_id=1, source_target_pairs={{0,7},{1,0},{2,1},{3,2},{4,3},{5,4},{6,5},{7,6},{8,15},{9,8},{10,9... | collective-permute-start | bytes 1671176 | tf_op jit(solution)/shard_map/ppermute | solution.py:32
  50.3 5.4 %collective-permute-done.6.refs_1_ = bf16[272,1024]{1,0:T(8,128)(2,1)} collective-permute-done((bf16[272,1024]{1,0:T(8,128)(2,1)}, bf16[272,1024]{1,0:T(8,128)(2,1)}, u32[]{:S(2)}, u32[]{:S(2)}) %collective-permute-start.6) | collective-permute-done | bytes 557088 | tf_op jit(solution)/shard_map/ppermute | solution.py:32
  55.7 5.3 %collective-permute-start.7 = (bf16[272,1024]{1,0:T(8,128)(2,1)}, bf16[272,1024]{1,0:T(8,128)(2,1)}, u32[]{:S(2)}, u32[]{:S(2)}) collective-permute-start(bf16[272,1024]{1,0:T(8,128)(2,1)} %collective-permute-done.6.refs_1_), channel_id=1, source_target_pairs={{0,7},{1,0},{2,1},{3,2},{4,3},{5,4},{6,5},{7,6},{8,15},{9,8},{10,9... | collective-permute-start | bytes 1671176 | tf_op jit(solution)/shard_map/ppermute | solution.py:32
  65.4 5.3 %collective-permute-start = (bf16[128,8192]{1,0:T(8,128)(2,1)}, bf16[128,8192]{1,0:T(8,128)(2,1)}, u32[]{:S(2)}, u32[]{:S(2)}) collective-permute-start(bf16[128,8192]{1,0:T(8,128)(2,1)} %bitcast.31), channel_id=1, source_target_pairs={{0,32},{32,0},{1,33},{33,1},{2,34},{34,2},{3,35},{35,3},{4,36},{36... | collective-permute-start | bytes 6291464 | tf_op jit(solution)/shard_map/ppermute | solution.py:36
  70.7 3.4 %products.4 = (bf16[8,64,2048]{2,1,0:T(8,128)(2,1)}, bf16[3,16,1024]{2,1,0:T(8,128)(2,1)}) custom-call(bf16[4,128,1024]{2,1,0:T(8,128)(2,1)S(1)} %all-to-all-done.masked_ref, bf16[272,1024]{1,0:T(8,128)(2,1)} %get-tuple-element.27.refs_0_, bf16[272,1024]{1,0:T(8,128)(2,1)} %collective-permute-done.1.refs_1_, bf16[272,1024]{1,0:T(8,128)(2,1)} %collective-permute-done.5.refs_2_), custom_call_target="tpu_custom_call" | custom-call | flops 805306368 | bytes 2097152 | tf_op jit(solution)/shard_map/products/pallas_call | solution.py:108
  81.9 6.5 %all-to-all-start.2 = ((bf16[8,64,2048]{2,1,0:T(8,128)(2,1)}), bf16[8,64,2048]{2,1,0:T(8,128)(2,1)}, u32[]{:S(2)}, u32[]{:S(2)}) async-start(bf16[8,64,2048]{2,1,0:T(8,128)(2,1)} %get-tuple-element.31.refs_0_.refs_4_), calls=%async_computation.2 | async-start | bytes 4194304 | tf_op jit(solution)/shard_map/all_to_all | solution.py:27
  96.3 18.4 %all-to-all-done.2.piece_ref = bf16[8,64,2048]{2,1,0:T(8,128)(2,1)} async-done(((bf16[8,64,2048]{2,1,0:T(8,128)(2,1)}), bf16[8,64,2048]{2,1,0:T(8,128)(2,1)}, u32[]{:S(2)}, u32[]{:S(2)}) %all-to-all-start.2) | async-done | bytes 2097184 | tf_op jit(solution)/shard_map/all_to_all | solution.py:27
  114.7 6.2 %norm_backward.1 = (bf16[64,8192]{1,0:T(8,128)(2,1)}, bf16[64,8192]{1,0:T(8,128)(2,1)}, bf16[64,8192]{1,0:T(8,128)(2,1)}) custom-call(s32[2]{0:T(128)S(1)} %pad_add_fusion.place_ref, bf16[128,8192]{1,0:T(8,128)(2,1)} %bitcast.33, bf16[128,8192]{1,0:T(8,128)(2,1)} %collective-permute-done.other_ref, f32[2,64,128]{2,1,0:T(8,128)S(1)} %inverses.1.inv_ref, ...), custom_call_target="tpu_custom_call" | custom-call | flops 20971520 | bytes 8388608 | tf_op jit(solution)/shard_map/norm_backward/pallas_call | solution.py:200
  121.0 6.9 %all-to-all-start.3 = ((bf16[8,8,8192]{2,1,0:T(8,128)(2,1)}), bf16[8,8,8192]{2,1,0:T(8,128)(2,1)S(1)}, u32[]{:S(2)}, u32[]{:S(2)}) async-start(bf16[8,8,8192]{2,1,0:T(8,128)(2,1)} %bitcast.35), calls=%async_computation.3 | async-start | bytes 2097152 | tf_op jit(solution)/shard_map/all_to_all | solution.py:27
  130.4 4.3 %collective-permute-start.8 = (bf16[64,512]{1,0:T(8,128)(2,1)S(1)}, bf16[64,512]{1,0:T(8,128)(2,1)S(1)}, u32[]{:S(2)}, u32[]{:S(2)}) collective-permute-start(bf16[64,512]{1,0:T(8,128)(2,1)S(1)} %copy-done.6), channel_id=1, source_target_pairs={{0,24},{8,0},{16,8},{24,16},{1,25},{9,1},{17,9},{25,17},{2,26},{10... | collective-permute-start | bytes 196616 | tf_op jit(solution)/shard_map/ppermute | solution.py:32
  136.7 4.5 %collective-permute-done.9.refs_2_ = bf16[64,512]{1,0:T(8,128)(2,1)S(1)} collective-permute-done((bf16[64,512]{1,0:T(8,128)(2,1)S(1)}, bf16[64,512]{1,0:T(8,128)(2,1)S(1)}, u32[]{:S(2)}, u32[]{:S(2)}) %collective-permute-start.9) | collective-permute-done | bytes 65568 | tf_op jit(solution)/shard_map/ppermute | solution.py:32
  141.8 3.6 %collective-permute-start.11 = (bf16[4,72,256]{2,1,0:T(8,128)(2,1)S(1)}, bf16[4,72,256]{2,1,0:T(8,128)(2,1)S(1)}, u32[]{:S(2)}, u32[]{:S(2)}) collective-permute-start(bf16[4,72,256]{2,1,0:T(8,128)(2,1)S(1)} %get-tuple-element.40), channel_id=1, source_target_pairs={{0,4},{1,5},{2,6},{3,7},{4,0},{5,1},{6,2},{7,3},{8,12},{9,13},{10,... | collective-permute-start | bytes 442376 | tf_op jit(solution)/shard_map/ppermute | solution.py:36
  145.5 8.6 %collective-permute-done.11.refs_1_ = bf16[4,72,256]{2,1,0:T(8,128)(2,1)S(1)} collective-permute-done((bf16[4,72,256]{2,1,0:T(8,128)(2,1)S(1)}, bf16[4,72,256]{2,1,0:T(8,128)(2,1)S(1)}, u32[]{:S(2)}, u32[]{:S(2)}) %collective-permute-start.11) | collective-permute-done | bytes 147488 | tf_op jit(solution)/shard_map/ppermute | solution.py:36
  158.3 3.6 %all-to-all-start.4 = ((bf16[8,8,8192]{2,1,0:T(8,128)(2,1)}), bf16[8,8,8192]{2,1,0:T(8,128)(2,1)S(1)}, u32[]{:S(2)}, u32[]{:S(2)}) async-start(bf16[8,8,8192]{2,1,0:T(8,128)(2,1)} %sums_above.1), calls=%async_computation.4 | async-start | bytes 2097152 | tf_op jit(solution)/shard_map/all_to_all | solution.py:27
  163.8 4.1 %collective-permute-done.12.refs_1_ = bf16[2,72,256]{2,1,0:T(8,128)(2,1)S(1)} collective-permute-done((bf16[2,72,256]{2,1,0:T(8,128)(2,1)S(1)}, bf16[2,72,256]{2,1,0:T(8,128)(2,1)S(1)}, u32[]{:S(2)}, u32[]{:S(2)}) %collective-permute-start.12) | collective-permute-done | bytes 73760 | tf_op jit(solution)/shard_map/ppermute | solution.py:36
  169.9 3.1 %collective-permute-done.13.refs_1_ = bf16[1,72,256]{2,1,0:T(8,128)(2,1)S(1)} collective-permute-done((bf16[1,72,256]{2,1,0:T(8,128)(2,1)S(1)}, bf16[1,72,256]{2,1,0:T(8,128)(2,1)S(1)}, u32[]{:S(2)}, u32[]{:S(2)}) %collective-permute-start.13) | collective-permute-done | bytes 36896 | tf_op jit(solution)/shard_map/ppermute | solution.py:36
  173.0 5.7 %collective-permute-start.15 = (bf16[64,8192]{1,0:T(8,128)(2,1)}, bf16[64,8192]{1,0:T(8,128)(2,1)S(1)}, u32[]{:S(2)}, u32[]{:S(2)}) collective-permute-start(bf16[64,8192]{1,0:T(8,128)(2,1)} %get-tuple-element.46), channel_id=1, source_target_pairs={{0,32},{32,0},{1,33},{33,1},{2,34},{34,2},{3,35},{35,3},{4,36},{36... | collective-permute-start | bytes 3145736 | tf_op jit(solution)/shard_map/ppermute | solution.py:36
  178.6 12.3 %all-to-all-done.4 = bf16[8,8,8192]{2,1,0:T(8,128)(2,1)S(1)} async-done(((bf16[8,8,8192]{2,1,0:T(8,128)(2,1)}), bf16[8,8,8192]{2,1,0:T(8,128)(2,1)S(1)}, u32[]{:S(2)}, u32[]{:S(2)}) %all-to-all-start.4) | async-done | bytes 1048608 | tf_op jit(solution)/shard_map/all_to_all | solution.py:27
  (60 shorter events, 50.4 us)
Async XLA Ops:
  0.6 33.7 %copy-start.1 = (f32[1,8192]{1,0:T(1,128)S(1)}, f32[1,8192]{1,0:T(1,128)}, u32[]{:S(2)}) copy-start(f32[1,8192]{1,0:T(1,128)} %gain_ref.1) | copy-start | bytes 98308
  4.6 32.8 %all-to-all-start = ((bf16[4,128,1024]{2,1,0:T(8,128)(2,1)}), bf16[4,128,1024]{2,1,0:T(8,128)(2,1)S(1)}, u32[]{:S(2)}, u32[]{:S(2)}) async-start(bf16[4,128,1024]{2,1,0:T(8,128)(2,1)} %get-tuple-element.26), calls=%async_computation | async-start | bytes 2097152 | tf_op jit(solution)/shard_map/all_to_all | solution.py:27
  9.4 23.0 %collective-permute-start.1 = (bf16[272,1024]{1,0:T(8,128)(2,1)}, bf16[272,1024]{1,0:T(8,128)(2,1)}, u32[]{:S(2)}, u32[]{:S(2)}) collective-permute-start(bf16[272,1024]{1,0:T(8,128)(2,1)} %get-tuple-element.27.refs_0_), channel_id=1, source_target_pairs={{0,1},{1,2},{2,3},{3,4},{4,5},{5,6},{6,7},{7,0},{8,9},{9,10},{10,1... | collective-permute-start | bytes 1671176 | tf_op jit(solution)/shard_map/ppermute | solution.py:32
  13.4 27.9 %collective-permute-start.5 = (bf16[272,1024]{1,0:T(8,128)(2,1)}, bf16[272,1024]{1,0:T(8,128)(2,1)}, u32[]{:S(2)}, u32[]{:S(2)}) collective-permute-start(bf16[272,1024]{1,0:T(8,128)(2,1)} %get-tuple-element.27.refs_0_), channel_id=1, source_target_pairs={{0,7},{1,0},{2,1},{3,2},{4,3},{5,4},{6,5},{7,6},{8,15},{9,8},{10,9... | collective-permute-start | bytes 1671176 | tf_op jit(solution)/shard_map/ppermute | solution.py:32
  32.4 16.0 %collective-permute-start.2 = (bf16[272,1024]{1,0:T(8,128)(2,1)}, bf16[272,1024]{1,0:T(8,128)(2,1)}, u32[]{:S(2)}, u32[]{:S(2)}) collective-permute-start(bf16[272,1024]{1,0:T(8,128)(2,1)} %collective-permute-done.1.refs_1_), channel_id=1, source_target_pairs={{0,1},{1,2},{2,3},{3,4},{4,5},{5,6},{6,7},{7,0},{8,9},{9,10},{10,1... | collective-permute-start | bytes 1671176 | tf_op jit(solution)/shard_map/ppermute | solution.py:32
  37.4 39.4 %all-to-all-start.1 = ((bf16[4,128,2048]{2,1,0:T(8,128)(2,1)}), bf16[4,128,2048]{2,1,0:T(8,128)(2,1)S(1)}, u32[]{:S(2)}, u32[]{:S(2)}) async-start(bf16[4,128,2048]{2,1,0:T(8,128)(2,1)} %normalise.1), calls=%async_computation.1 | async-start | bytes 4194304 | tf_op jit(solution)/shard_map/all_to_all | solution.py:27
  41.4 14.4 %collective-permute-start.6 = (bf16[272,1024]{1,0:T(8,128)(2,1)}, bf16[272,1024]{1,0:T(8,128)(2,1)}, u32[]{:S(2)}, u32[]{:S(2)}) collective-permute-start(bf16[272,1024]{1,0:T(8,128)(2,1)} %collective-permute-done.5.refs_2_), channel_id=1, source_target_pairs={{0,7},{1,0},{2,1},{3,2},{4,3},{5,4},{6,5},{7,6},{8,15},{9,8},{10,9... | collective-permute-start | bytes 1671176 | tf_op jit(solution)/shard_map/ppermute | solution.py:32
  48.4 15.1 %collective-permute-start.3 = (bf16[272,1024]{1,0:T(8,128)(2,1)}, bf16[272,1024]{1,0:T(8,128)(2,1)}, u32[]{:S(2)}, u32[]{:S(2)}) collective-permute-start(bf16[272,1024]{1,0:T(8,128)(2,1)} %collective-permute-done.2.refs_0_), channel_id=1, source_target_pairs={{0,1},{1,2},{2,3},{3,4},{4,5},{5,6},{6,7},{7,0},{8,9},{9,10},{10,1... | collective-permute-start | bytes 1671176 | tf_op jit(solution)/shard_map/ppermute | solution.py:32
  55.7 21.2 %collective-permute-start.7 = (bf16[272,1024]{1,0:T(8,128)(2,1)}, bf16[272,1024]{1,0:T(8,128)(2,1)}, u32[]{:S(2)}, u32[]{:S(2)}) collective-permute-start(bf16[272,1024]{1,0:T(8,128)(2,1)} %collective-permute-done.6.refs_1_), channel_id=1, source_target_pairs={{0,7},{1,0},{2,1},{3,2},{4,3},{5,4},{6,5},{7,6},{8,15},{9,8},{10,9... | collective-permute-start | bytes 1671176 | tf_op jit(solution)/shard_map/ppermute | solution.py:32
  63.5 16.2 %collective-permute-start.4 = (bf16[272,1024]{1,0:T(8,128)(2,1)}, bf16[272,1024]{1,0:T(8,128)(2,1)}, u32[]{:S(2)}, u32[]{:S(2)}) collective-permute-start(bf16[272,1024]{1,0:T(8,128)(2,1)} %collective-permute-done.3.refs_0_), channel_id=1, source_target_pairs={{0,1},{1,2},{2,3},{3,4},{4,5},{5,6},{6,7},{7,0},{8,9},{9,10},{10,1... | collective-permute-start | bytes 1671176 | tf_op jit(solution)/shard_map/ppermute | solution.py:32
  65.4 25.0 %collective-permute-start = (bf16[128,8192]{1,0:T(8,128)(2,1)}, bf16[128,8192]{1,0:T(8,128)(2,1)}, u32[]{:S(2)}, u32[]{:S(2)}) collective-permute-start(bf16[128,8192]{1,0:T(8,128)(2,1)} %bitcast.31), channel_id=1, source_target_pairs={{0,32},{32,0},{1,33},{33,1},{2,34},{34,2},{3,35},{35,3},{4,36},{36... | collective-permute-start | bytes 6291464 | tf_op jit(solution)/shard_map/ppermute | solution.py:36
  81.9 32.8 %all-to-all-start.2 = ((bf16[8,64,2048]{2,1,0:T(8,128)(2,1)}), bf16[8,64,2048]{2,1,0:T(8,128)(2,1)}, u32[]{:S(2)}, u32[]{:S(2)}) async-start(bf16[8,64,2048]{2,1,0:T(8,128)(2,1)} %get-tuple-element.31.refs_0_.refs_4_), calls=%async_computation.2 | async-start | bytes 4194304 | tf_op jit(solution)/shard_map/all_to_all | solution.py:27
  120.9 6.9 %copy-start.6 = (bf16[64,512]{1,0:T(8,128)(2,1)S(1)}, bf16[64,512]{1,0:T(8,128)(2,1)}, u32[]{:S(2)}) copy-start(bf16[64,512]{1,0:T(8,128)(2,1)} %copy-done.5) | copy-start | bytes 196612
  121.0 36.2 %all-to-all-start.3 = ((bf16[8,8,8192]{2,1,0:T(8,128)(2,1)}), bf16[8,8,8192]{2,1,0:T(8,128)(2,1)S(1)}, u32[]{:S(2)}, u32[]{:S(2)}) async-start(bf16[8,8,8192]{2,1,0:T(8,128)(2,1)} %bitcast.35), calls=%async_computation.3 | async-start | bytes 2097152 | tf_op jit(solution)/shard_map/all_to_all | solution.py:27
  127.9 8.8 %collective-permute-start.10 = (bf16[64,512]{1,0:T(8,128)(2,1)S(1)}, bf16[64,512]{1,0:T(8,128)(2,1)S(1)}, u32[]{:S(2)}, u32[]{:S(2)}) collective-permute-start(bf16[64,512]{1,0:T(8,128)(2,1)S(1)} %copy-done.6), channel_id=1, source_target_pairs={{0,16},{8,24},{16,0},{24,8},{1,17},{9,25},{17,1},{25,9},{2,18},{10... | collective-permute-start | bytes 196616 | tf_op jit(solution)/shard_map/ppermute | solution.py:32
  130.4 6.2 %collective-permute-start.8 = (bf16[64,512]{1,0:T(8,128)(2,1)S(1)}, bf16[64,512]{1,0:T(8,128)(2,1)S(1)}, u32[]{:S(2)}, u32[]{:S(2)}) collective-permute-start(bf16[64,512]{1,0:T(8,128)(2,1)S(1)} %copy-done.6), channel_id=1, source_target_pairs={{0,24},{8,0},{16,8},{24,16},{1,25},{9,1},{17,9},{25,17},{2,26},{10... | collective-permute-start | bytes 196616 | tf_op jit(solution)/shard_map/ppermute | solution.py:32
  134.7 6.5 %collective-permute-start.9 = (bf16[64,512]{1,0:T(8,128)(2,1)S(1)}, bf16[64,512]{1,0:T(8,128)(2,1)S(1)}, u32[]{:S(2)}, u32[]{:S(2)}) collective-permute-start(bf16[64,512]{1,0:T(8,128)(2,1)S(1)} %copy-done.6), channel_id=1, source_target_pairs={{0,8},{8,16},{16,24},{24,0},{1,9},{9,17},{17,25},{25,1},{2,10},{10... | collective-permute-start | bytes 196616 | tf_op jit(solution)/shard_map/ppermute | solution.py:32
  141.8 12.2 %collective-permute-start.11 = (bf16[4,72,256]{2,1,0:T(8,128)(2,1)S(1)}, bf16[4,72,256]{2,1,0:T(8,128)(2,1)S(1)}, u32[]{:S(2)}, u32[]{:S(2)}) collective-permute-start(bf16[4,72,256]{2,1,0:T(8,128)(2,1)S(1)} %get-tuple-element.40), channel_id=1, source_target_pairs={{0,4},{1,5},{2,6},{3,7},{4,0},{5,1},{6,2},{7,3},{8,12},{9,13},{10,... | collective-permute-start | bytes 442376 | tf_op jit(solution)/shard_map/ppermute | solution.py:36
  157.1 37.0 %copy-start = (bf16[64,8192]{1,0:T(8,128)(2,1)S(1)}, bf16[64,8192]{1,0:T(8,128)(2,1)}, u32[]{:S(2)}) copy-start(bf16[64,8192]{1,0:T(8,128)(2,1)} %get-tuple-element.47.sum_ref) | copy-start | bytes 3145732
  158.3 32.7 %all-to-all-start.4 = ((bf16[8,8,8192]{2,1,0:T(8,128)(2,1)}), bf16[8,8,8192]{2,1,0:T(8,128)(2,1)S(1)}, u32[]{:S(2)}, u32[]{:S(2)}) async-start(bf16[8,8,8192]{2,1,0:T(8,128)(2,1)} %sums_above.1), calls=%async_computation.4 | async-start | bytes 2097152 | tf_op jit(solution)/shard_map/all_to_all | solution.py:27
  161.8 6.1 %collective-permute-start.12 = (bf16[2,72,256]{2,1,0:T(8,128)(2,1)S(1)}, bf16[2,72,256]{2,1,0:T(8,128)(2,1)S(1)}, u32[]{:S(2)}, u32[]{:S(2)}) collective-permute-start(bf16[2,72,256]{2,1,0:T(8,128)(2,1)S(1)} %get-tuple-element.42), channel_id=1, source_target_pairs={{0,2},{1,3},{2,0},{3,1},{4,6},{5,7},{6,4},{7,5},{8,10},{9,11},{10,... | collective-permute-start | bytes 221192 | tf_op jit(solution)/shard_map/ppermute | solution.py:36
  168.0 5.0 %collective-permute-start.13 = (bf16[1,72,256]{2,1,0:T(8,128)(2,1)S(1)}, bf16[1,72,256]{2,1,0:T(8,128)(2,1)S(1)}, u32[]{:S(2)}, u32[]{:S(2)}) collective-permute-start(bf16[1,72,256]{2,1,0:T(8,128)(2,1)S(1)} %get-tuple-element.44), channel_id=1, source_target_pairs={{0,1},{1,0},{2,3},{3,2},{4,5},{5,4},{6,7},{7,6},{8,9},{9,8},{10,11... | collective-permute-start | bytes 110600 | tf_op jit(solution)/shard_map/ppermute | solution.py:36
  173.0 23.4 %collective-permute-start.15 = (bf16[64,8192]{1,0:T(8,128)(2,1)}, bf16[64,8192]{1,0:T(8,128)(2,1)S(1)}, u32[]{:S(2)}, u32[]{:S(2)}) collective-permute-start(bf16[64,8192]{1,0:T(8,128)(2,1)} %get-tuple-element.46), channel_id=1, source_target_pairs={{0,32},{32,0},{1,33},{33,1},{2,34},{34,2},{3,35},{35,3},{4,36},{36... | collective-permute-start | bytes 3145736 | tf_op jit(solution)/shard_map/ppermute | solution.py:36
  190.9 5.4 %collective-permute-start.14 = (bf16[64,8192]{1,0:T(8,128)(2,1)S(1)}, bf16[64,8192]{1,0:T(8,128)(2,1)}, u32[]{:S(2)}, u32[]{:S(2)}) collective-permute-start(bf16[64,8192]{1,0:T(8,128)(2,1)S(1)} %bitcast.25), channel_id=1, source_target_pairs={{0,32},{32,0},{1,33},{33,1},{2,34},{34,2},{3,35},{35,3},{4,36},{36... | collective-permute-start | bytes 3145736 | tf_op jit(solution)/shard_map/ppermute | solution.py:36
  (5 other events, 10.6 us)

commit v4 on v3

--- a/solution.py
+++ b/solution.py
@@ -87,22 +87,22 @@
 def products_kernel(share, count, masked_ref, *refs):
     blocks, (out_ref, a_ref) = refs[:count], refs[-2:]
     nx, tokens, key_width = masked_ref.shape
-    half = out_ref.shape[1]
+    half = out_ref.shape[2]
     rows = masked_ref[...].reshape(nx * tokens, key_width)
     for at, block in enumerate(blocks):
         columns = contract(rows, block[:share], (1, 1)).astype(BF16)
         for chip in range(nx):
             for part in range(tokens // half):
                 start = chip * tokens + part * half
-                out_ref[part * nx + chip, :, at * share : (at + 1) * share] = columns[start : start + half]
+                out_ref[part * nx + chip, at] = columns[start : start + half]
     for slot, block in enumerate(blocks):
         a_ref[slot] = block[share:]
 
 
-def products(masked_x, blocks, share, cores, width, column=0, into=None, after=()):
+def products(masked_x, blocks, share, cores, slots, slot=0, into=None, after=()):
     nx, tokens, key_width = masked_x.shape
-    columns = share * len(blocks)
-    shape = (cores * nx, tokens // cores, width)
+    count = len(blocks)
+    shape = (cores * nx, slots, tokens // cores, share)
     extra = list(after) + ([] if into is None else [into])
     a_shape = (len(blocks), blocks[0].shape[0] - share, key_width)
     return pl.pallas_call(
@@ -114,12 +114,12 @@
         + [ANY] * len(after)
         + [HBM] * (into is not None),
         out_specs=(
-            pl.BlockSpec(shape[:2] + (columns,), lambda i: (0, 0, column // columns)),
+            pl.BlockSpec((shape[0], count) + shape[2:], lambda i: (0, slot // count, 0, 0)),
             whole(*a_shape),
         ),
         input_output_aliases={} if into is None else {len(blocks) + len(extra): 0},
         compiler_params=params(20),
-        cost_estimate=cost(2 * masked_x.size * columns, 2 * masked_x.size),
+        cost_estimate=cost(2 * masked_x.size * share * count, 2 * masked_x.size),
         name="products",
     )(masked_x, *blocks, *extra)
 
@@ -164,22 +164,22 @@
         for at, offset in enumerate(offsets):
             slot = lax.rem(z + (offset + nz), nz)
             start = pl.multiple_of(chip * (nz * share) + slot * share, share)
-            columns.append((chip, slice(at * share, (at + 1) * share), pl.ds(start, share)))
+            columns.append((chip, at, pl.ds(start, share)))
 
     layers = ((own_ref, core), (other_ref, 1 - core))
     factors = []
     for index, (hidden_ref, layer) in enumerate(layers):
         partial = jnp.zeros((rows, share), F32)
-        for chip, cols, place in columns:
-            slope = gain_ref[layer, :, place] * piece_ref[layer * nx + chip, :, cols].astype(F32)
+        for chip, at, place in columns:
+            slope = gain_ref[layer, :, place] * piece_ref[layer * nx + chip, at].astype(F32)
             partial += hidden_ref[:, place].astype(F32) * slope
         inv = inv_ref[index, :, :1]
         inner = jnp.sum(partial, axis=1, keepdims=True) * (1.0 / width)
         factors.append((inv, inv * inv * inner))
-    for chip, cols, place in columns:
+    for chip, at, place in columns:
         terms = []
         for (hidden_ref, layer), (inv, factor) in zip(layers, factors):
-            slope = gain_ref[layer, :, place] * piece_ref[layer * nx + chip, :, cols].astype(F32)
+            slope = gain_ref[layer, :, place] * piece_ref[layer * nx + chip, at].astype(F32)
             terms.append((inv * (slope - hidden_ref[:, place].astype(F32) * factor)).astype(BF16))
         total = (terms[0].astype(F32) + terms[1].astype(F32)).astype(BF16)
         total_ref[:, place] = total
@@ -189,7 +189,7 @@
 
 def norm_backward(place, hidden, other, inv_pair, gain_pair, piece, offsets, after, share):
     half, width = other.shape[0] // 2, other.shape[1]
-    rows = 16
+    rows = 32
     steps = half // rows
     half_block = pl.BlockSpec((rows, width), lambda i, at: (at[1] * steps + i, 0))
     row_block = pl.BlockSpec((rows, width), lambda i, at: (i, 0))
@@ -202,7 +202,8 @@
         grid_spec=pltpu.PrefetchScalarGridSpec(
             num_scalar_prefetch=1,
             grid=(steps,),
-            in_specs=[half_block, half_block, by_rows(inv_pair), whole(*gain_pair.shape), by_rows(piece)]
+            in_specs=[half_block, half_block, by_rows(inv_pair), whole(*gain_pair.shape)]
+            + [pl.BlockSpec(piece.shape[:2] + (rows, share), lambda i, at: (0, 0, i, 0))]
             + [ANY] * len(after),
             out_specs=(row_block,) * 3,
         ),
@@ -476,8 +477,8 @@
             blocks,
             share,
             cores,
-            nz * share,
-            column=slot * share,
+            nz,
+            slot,
             into=dnorm,
             after=[normed_x] if slot == 6 else [],
         )

time: 201 us -> 200 us (level)
  no operation moved by 1% of the time
where the time goes in v4:
time: 200 us; the launch traced here: 199 us
  starting transfers between devices  83.5 us (42%)
  waiting for transfers between devices  74.8 us (37%)
  Pallas kernels  33.6 us (17%)
  local copies, waits for them, and re-layouts  2.42 us (1%)
  between operations  2.3 us (1%)
    ppermute x10, starting transfers between devices, shift(): lax.ppermute(value, axis, [(i, (i + by) % size) for i in range(size)])  36.9 us
    all_to_all x5, waiting for transfers between devices, exchange(): return lax.all_to_all(value, axes, 0, 0, tiled=True)  33.6 us
    all_to_all x5, starting transfers between devices, exchange(): return lax.all_to_all(value, axes, 0, 0, tiled=True)  25.8 us
    ppermute x10, waiting for transfers between devices, shift(): lax.ppermute(value, axis, [(i, (i + by) % size) for i in range(size)])  25.3 us
    ppermute x6, starting transfers between devices, swap(): lax.ppermute(value, axis, [(i, i ^ bit) for i in range(lax.axis_size(axis...  20.8 us
    ppermute x6, waiting for transfers between devices, swap(): lax.ppermute(value, axis, [(i, i ^ bit) for i in range(lax.axis_size(axis...  16 us
    pallas_call x4, Pallas kernels, products(): pl.pallas_call(functools.partial(products_kernel, share, len(blocks)), gr...  11.1 us
    pallas_call x1, Pallas kernels, norm_backward(): pl.pallas_call(functools.partial(term_kernel, share, offsets), grid_spec=...  5.62 us
  transfers between devices with their start and end apart: 21, of which 11 were waited for; matrix products, arithmetic and copies ran while one was open for 1% of the time, Pallas kernels for 11%

profile of v4, /device:TPU:1, one launch (start us, length us, event | category | flops | bytes accessed | tf_op | source)
XLA Modules:
  0.0 198.7 jit_solution(10684730698994265464)
XLA Ops:
  4.6 4.8 %all-to-all-start = ((bf16[4,128,1024]{2,1,0:T(8,128)(2,1)}), bf16[4,128,1024]{2,1,0:T(8,128)(2,1)S(1)}, u32[]{:S(2)}, u32[]{:S(2)}) async-start(bf16[4,128,1024]{2,1,0:T(8,128)(2,1)} %get-tuple-element.26), calls=%async_computation | async-start | bytes 2097152 | tf_op jit(solution)/shard_map/all_to_all | solution.py:27
  9.4 4.0 %collective-permute-start.1 = (bf16[272,1024]{1,0:T(8,128)(2,1)}, bf16[272,1024]{1,0:T(8,128)(2,1)}, u32[]{:S(2)}, u32[]{:S(2)}) collective-permute-start(bf16[272,1024]{1,0:T(8,128)(2,1)} %get-tuple-element.27.refs_0_), channel_id=1, source_target_pairs={{0,1},{1,2},{2,3},{3,4},{4,5},{5,6},{6,7},{7,0},{8,9},{9,10},{10,1... | collective-permute-start | bytes 1671176 | tf_op jit(solution)/shard_map/ppermute | solution.py:32
  13.4 8.6 %collective-permute-start.5 = (bf16[272,1024]{1,0:T(8,128)(2,1)}, bf16[272,1024]{1,0:T(8,128)(2,1)}, u32[]{:S(2)}, u32[]{:S(2)}) collective-permute-start(bf16[272,1024]{1,0:T(8,128)(2,1)} %get-tuple-element.27.refs_0_), channel_id=1, source_target_pairs={{0,7},{1,0},{2,1},{3,2},{4,3},{5,4},{6,5},{7,6},{8,15},{9,8},{10,9... | collective-permute-start | bytes 1671176 | tf_op jit(solution)/shard_map/ppermute | solution.py:32
  22.0 10.4 %collective-permute-done.1.refs_1_ = bf16[272,1024]{1,0:T(8,128)(2,1)} collective-permute-done((bf16[272,1024]{1,0:T(8,128)(2,1)}, bf16[272,1024]{1,0:T(8,128)(2,1)}, u32[]{:S(2)}, u32[]{:S(2)}) %collective-permute-start.1) | collective-permute-done | bytes 557088 | tf_op jit(solution)/shard_map/ppermute | solution.py:32
  34.4 3.1 %normalise.1 = bf16[4,128,2048]{2,1,0:T(8,128)(2,1)} custom-call(bf16[128,8192]{1,0:T(8,128)(2,1)} %bitcast.30, f32[1,8192]{1,0:T(1,128)S(1)} %copy-done.1), custom_call_target="tpu_custom_call" | custom-call | flops 6291456 | bytes 4194304 | tf_op jit(solution)/shard_map/normalise/pallas_call | solution.py:293
  37.4 3.9 %all-to-all-start.1 = ((bf16[4,128,2048]{2,1,0:T(8,128)(2,1)}), bf16[4,128,2048]{2,1,0:T(8,128)(2,1)S(1)}, u32[]{:S(2)}, u32[]{:S(2)}) async-start(bf16[4,128,2048]{2,1,0:T(8,128)(2,1)} %normalise.1), calls=%async_computation.1 | async-start | bytes 4194304 | tf_op jit(solution)/shard_map/all_to_all | solution.py:27
  41.4 4.6 %collective-permute-start.6 = (bf16[272,1024]{1,0:T(8,128)(2,1)}, bf16[272,1024]{1,0:T(8,128)(2,1)}, u32[]{:S(2)}, u32[]{:S(2)}) collective-permute-start(bf16[272,1024]{1,0:T(8,128)(2,1)} %collective-permute-done.5.refs_2_), channel_id=1, source_target_pairs={{0,7},{1,0},{2,1},{3,2},{4,3},{5,4},{6,5},{7,6},{8,15},{9,8},{10,9... | collective-permute-start | bytes 1671176 | tf_op jit(solution)/shard_map/ppermute | solution.py:32
  50.3 5.4 %collective-permute-done.6.refs_1_ = bf16[272,1024]{1,0:T(8,128)(2,1)} collective-permute-done((bf16[272,1024]{1,0:T(8,128)(2,1)}, bf16[272,1024]{1,0:T(8,128)(2,1)}, u32[]{:S(2)}, u32[]{:S(2)}) %collective-permute-start.6) | collective-permute-done | bytes 557088 | tf_op jit(solution)/shard_map/ppermute | solution.py:32
  55.7 5.3 %collective-permute-start.7 = (bf16[272,1024]{1,0:T(8,128)(2,1)}, bf16[272,1024]{1,0:T(8,128)(2,1)}, u32[]{:S(2)}, u32[]{:S(2)}) collective-permute-start(bf16[272,1024]{1,0:T(8,128)(2,1)} %collective-permute-done.6.refs_1_), channel_id=1, source_target_pairs={{0,7},{1,0},{2,1},{3,2},{4,3},{5,4},{6,5},{7,6},{8,15},{9,8},{10,9... | collective-permute-start | bytes 1671176 | tf_op jit(solution)/shard_map/ppermute | solution.py:32
  65.4 5.3 %collective-permute-start = (bf16[128,8192]{1,0:T(8,128)(2,1)}, bf16[128,8192]{1,0:T(8,128)(2,1)}, u32[]{:S(2)}, u32[]{:S(2)}) collective-permute-start(bf16[128,8192]{1,0:T(8,128)(2,1)} %bitcast.31), channel_id=1, source_target_pairs={{0,32},{32,0},{1,33},{33,1},{2,34},{34,2},{3,35},{35,3},{4,36},{36... | collective-permute-start | bytes 6291464 | tf_op jit(solution)/shard_map/ppermute | solution.py:36
  70.7 3.3 %products.4 = (bf16[8,8,64,256]{3,2,1,0:T(8,128)(2,1)}, bf16[3,16,1024]{2,1,0:T(8,128)(2,1)}) custom-call(bf16[4,128,1024]{2,1,0:T(8,128)(2,1)S(1)} %all-to-all-done.masked_ref, bf16[272,1024]{1,0:T(8,128)(2,1)} %get-tuple-element.27.refs_0_, bf16[272,1024]{1,0:T(8,128)(2,1)} %collective-permute-done.1.refs_1_, bf16[272,1024]{1,0:T(8,128)(2,1)} %collective-permute-done.5.refs_2_), custom_call_target="tpu_custom_call" | custom-call | flops 805306368 | bytes 2097152 | tf_op jit(solution)/shard_map/products/pallas_call | solution.py:108
  81.9 6.6 %all-to-all-start.2 = ((bf16[8,8,64,256]{3,2,1,0:T(8,128)(2,1)}), bf16[8,8,64,256]{3,2,1,0:T(8,128)(2,1)}, u32[]{:S(2)}, u32[]{:S(2)}) async-start(bf16[8,8,64,256]{3,2,1,0:T(8,128)(2,1)} %get-tuple-element.31.refs_0_.refs_4_), calls=%async_computation.2 | async-start | bytes 4194304 | tf_op jit(solution)/shard_map/all_to_all | solution.py:27
  96.3 18.4 %all-to-all-done.2.piece_ref = bf16[8,8,64,256]{3,2,1,0:T(8,128)(2,1)} async-done(((bf16[8,8,64,256]{3,2,1,0:T(8,128)(2,1)}), bf16[8,8,64,256]{3,2,1,0:T(8,128)(2,1)}, u32[]{:S(2)}, u32[]{:S(2)}) %all-to-all-start.2) | async-done | bytes 2097184 | tf_op jit(solution)/shard_map/all_to_all | solution.py:27
  114.8 5.6 %norm_backward.1 = (bf16[64,8192]{1,0:T(8,128)(2,1)}, bf16[64,8192]{1,0:T(8,128)(2,1)}, bf16[64,8192]{1,0:T(8,128)(2,1)}) custom-call(s32[2]{0:T(128)S(1)} %pad_add_fusion.place_ref, bf16[128,8192]{1,0:T(8,128)(2,1)} %bitcast.33, bf16[128,8192]{1,0:T(8,128)(2,1)} %collective-permute-done.other_ref, f32[2,64,128]{2,1,0:T(8,128)S(1)} %inverses.1.inv_ref, ...), custom_call_target="tpu_custom_call" | custom-call | flops 20971520 | bytes 8388608 | tf_op jit(solution)/shard_map/norm_backward/pallas_call | solution.py:200
  120.4 6.9 %all-to-all-start.3 = ((bf16[8,8,8192]{2,1,0:T(8,128)(2,1)}), bf16[8,8,8192]{2,1,0:T(8,128)(2,1)S(1)}, u32[]{:S(2)}, u32[]{:S(2)}) async-start(bf16[8,8,8192]{2,1,0:T(8,128)(2,1)} %bitcast.35), calls=%async_computation.3 | async-start | bytes 2097152 | tf_op jit(solution)/shard_map/all_to_all | solution.py:27
  129.9 4.3 %collective-permute-start.8 = (bf16[64,512]{1,0:T(8,128)(2,1)S(1)}, bf16[64,512]{1,0:T(8,128)(2,1)S(1)}, u32[]{:S(2)}, u32[]{:S(2)}) collective-permute-start(bf16[64,512]{1,0:T(8,128)(2,1)S(1)} %copy-done.6), channel_id=1, source_target_pairs={{0,24},{8,0},{16,8},{24,16},{1,25},{9,1},{17,9},{25,17},{2,26},{10... | collective-permute-start | bytes 196616 | tf_op jit(solution)/shard_map/ppermute | solution.py:32
  136.1 4.5 %collective-permute-done.9.refs_2_ = bf16[64,512]{1,0:T(8,128)(2,1)S(1)} collective-permute-done((bf16[64,512]{1,0:T(8,128)(2,1)S(1)}, bf16[64,512]{1,0:T(8,128)(2,1)S(1)}, u32[]{:S(2)}, u32[]{:S(2)}) %collective-permute-start.9) | collective-permute-done | bytes 65568 | tf_op jit(solution)/shard_map/ppermute | solution.py:32
  141.3 3.6 %collective-permute-start.11 = (bf16[4,72,256]{2,1,0:T(8,128)(2,1)S(1)}, bf16[4,72,256]{2,1,0:T(8,128)(2,1)S(1)}, u32[]{:S(2)}, u32[]{:S(2)}) collective-permute-start(bf16[4,72,256]{2,1,0:T(8,128)(2,1)S(1)} %get-tuple-element.40), channel_id=1, source_target_pairs={{0,4},{1,5},{2,6},{3,7},{4,0},{5,1},{6,2},{7,3},{8,12},{9,13},{10,... | collective-permute-start | bytes 442376 | tf_op jit(solution)/shard_map/ppermute | solution.py:36
  144.9 8.7 %collective-permute-done.11.refs_1_ = bf16[4,72,256]{2,1,0:T(8,128)(2,1)S(1)} collective-permute-done((bf16[4,72,256]{2,1,0:T(8,128)(2,1)S(1)}, bf16[4,72,256]{2,1,0:T(8,128)(2,1)S(1)}, u32[]{:S(2)}, u32[]{:S(2)}) %collective-permute-start.11) | collective-permute-done | bytes 147488 | tf_op jit(solution)/shard_map/ppermute | solution.py:36
  157.7 3.6 %all-to-all-start.4 = ((bf16[8,8,8192]{2,1,0:T(8,128)(2,1)}), bf16[8,8,8192]{2,1,0:T(8,128)(2,1)S(1)}, u32[]{:S(2)}, u32[]{:S(2)}) async-start(bf16[8,8,8192]{2,1,0:T(8,128)(2,1)} %sums_above.1), calls=%async_computation.4 | async-start | bytes 2097152 | tf_op jit(solution)/shard_map/all_to_all | solution.py:27
  163.2 4.2 %collective-permute-done.12.refs_1_ = bf16[2,72,256]{2,1,0:T(8,128)(2,1)S(1)} collective-permute-done((bf16[2,72,256]{2,1,0:T(8,128)(2,1)S(1)}, bf16[2,72,256]{2,1,0:T(8,128)(2,1)S(1)}, u32[]{:S(2)}, u32[]{:S(2)}) %collective-permute-start.12) | collective-permute-done | bytes 73760 | tf_op jit(solution)/shard_map/ppermute | solution.py:36
  169.4 3.1 %collective-permute-done.13.refs_1_ = bf16[1,72,256]{2,1,0:T(8,128)(2,1)S(1)} collective-permute-done((bf16[1,72,256]{2,1,0:T(8,128)(2,1)S(1)}, bf16[1,72,256]{2,1,0:T(8,128)(2,1)S(1)}, u32[]{:S(2)}, u32[]{:S(2)}) %collective-permute-start.13) | collective-permute-done | bytes 36896 | tf_op jit(solution)/shard_map/ppermute | solution.py:36
  172.5 5.7 %collective-permute-start.15 = (bf16[64,8192]{1,0:T(8,128)(2,1)}, bf16[64,8192]{1,0:T(8,128)(2,1)S(1)}, u32[]{:S(2)}, u32[]{:S(2)}) collective-permute-start(bf16[64,8192]{1,0:T(8,128)(2,1)} %get-tuple-element.46), channel_id=1, source_target_pairs={{0,32},{32,0},{1,33},{33,1},{2,34},{34,2},{3,35},{35,3},{4,36},{36... | collective-permute-start | bytes 3145736 | tf_op jit(solution)/shard_map/ppermute | solution.py:36
  178.1 12.2 %all-to-all-done.4 = bf16[8,8,8192]{2,1,0:T(8,128)(2,1)S(1)} async-done(((bf16[8,8,8192]{2,1,0:T(8,128)(2,1)}), bf16[8,8,8192]{2,1,0:T(8,128)(2,1)S(1)}, u32[]{:S(2)}, u32[]{:S(2)}) %all-to-all-start.4) | async-done | bytes 1048608 | tf_op jit(solution)/shard_map/all_to_all | solution.py:27
  (60 shorter events, 50.2 us)
Async XLA Ops:
  0.6 33.7 %copy-start.1 = (f32[1,8192]{1,0:T(1,128)S(1)}, f32[1,8192]{1,0:T(1,128)}, u32[]{:S(2)}) copy-start(f32[1,8192]{1,0:T(1,128)} %gain_ref.1) | copy-start | bytes 98308
  4.6 32.8 %all-to-all-start = ((bf16[4,128,1024]{2,1,0:T(8,128)(2,1)}), bf16[4,128,1024]{2,1,0:T(8,128)(2,1)S(1)}, u32[]{:S(2)}, u32[]{:S(2)}) async-start(bf16[4,128,1024]{2,1,0:T(8,128)(2,1)} %get-tuple-element.26), calls=%async_computation | async-start | bytes 2097152 | tf_op jit(solution)/shard_map/all_to_all | solution.py:27
  9.4 23.0 %collective-permute-start.1 = (bf16[272,1024]{1,0:T(8,128)(2,1)}, bf16[272,1024]{1,0:T(8,128)(2,1)}, u32[]{:S(2)}, u32[]{:S(2)}) collective-permute-start(bf16[272,1024]{1,0:T(8,128)(2,1)} %get-tuple-element.27.refs_0_), channel_id=1, source_target_pairs={{0,1},{1,2},{2,3},{3,4},{4,5},{5,6},{6,7},{7,0},{8,9},{9,10},{10,1... | collective-permute-start | bytes 1671176 | tf_op jit(solution)/shard_map/ppermute | solution.py:32
  13.4 27.9 %collective-permute-start.5 = (bf16[272,1024]{1,0:T(8,128)(2,1)}, bf16[272,1024]{1,0:T(8,128)(2,1)}, u32[]{:S(2)}, u32[]{:S(2)}) collective-permute-start(bf16[272,1024]{1,0:T(8,128)(2,1)} %get-tuple-element.27.refs_0_), channel_id=1, source_target_pairs={{0,7},{1,0},{2,1},{3,2},{4,3},{5,4},{6,5},{7,6},{8,15},{9,8},{10,9... | collective-permute-start | bytes 1671176 | tf_op jit(solution)/shard_map/ppermute | solution.py:32
  32.4 16.0 %collective-permute-start.2 = (bf16[272,1024]{1,0:T(8,128)(2,1)}, bf16[272,1024]{1,0:T(8,128)(2,1)}, u32[]{:S(2)}, u32[]{:S(2)}) collective-permute-start(bf16[272,1024]{1,0:T(8,128)(2,1)} %collective-permute-done.1.refs_1_), channel_id=1, source_target_pairs={{0,1},{1,2},{2,3},{3,4},{4,5},{5,6},{6,7},{7,0},{8,9},{9,10},{10,1... | collective-permute-start | bytes 1671176 | tf_op jit(solution)/shard_map/ppermute | solution.py:32
  37.4 39.4 %all-to-all-start.1 = ((bf16[4,128,2048]{2,1,0:T(8,128)(2,1)}), bf16[4,128,2048]{2,1,0:T(8,128)(2,1)S(1)}, u32[]{:S(2)}, u32[]{:S(2)}) async-start(bf16[4,128,2048]{2,1,0:T(8,128)(2,1)} %normalise.1), calls=%async_computation.1 | async-start | bytes 4194304 | tf_op jit(solution)/shard_map/all_to_all | solution.py:27
  41.4 14.4 %collective-permute-start.6 = (bf16[272,1024]{1,0:T(8,128)(2,1)}, bf16[272,1024]{1,0:T(8,128)(2,1)}, u32[]{:S(2)}, u32[]{:S(2)}) collective-permute-start(bf16[272,1024]{1,0:T(8,128)(2,1)} %collective-permute-done.5.refs_2_), channel_id=1, source_target_pairs={{0,7},{1,0},{2,1},{3,2},{4,3},{5,4},{6,5},{7,6},{8,15},{9,8},{10,9... | collective-permute-start | bytes 1671176 | tf_op jit(solution)/shard_map/ppermute | solution.py:32
  48.4 15.1 %collective-permute-start.3 = (bf16[272,1024]{1,0:T(8,128)(2,1)}, bf16[272,1024]{1,0:T(8,128)(2,1)}, u32[]{:S(2)}, u32[]{:S(2)}) collective-permute-start(bf16[272,1024]{1,0:T(8,128)(2,1)} %collective-permute-done.2.refs_0_), channel_id=1, source_target_pairs={{0,1},{1,2},{2,3},{3,4},{4,5},{5,6},{6,7},{7,0},{8,9},{9,10},{10,1... | collective-permute-start | bytes 1671176 | tf_op jit(solution)/shard_map/ppermute | solution.py:32
  55.7 21.1 %collective-permute-start.7 = (bf16[272,1024]{1,0:T(8,128)(2,1)}, bf16[272,1024]{1,0:T(8,128)(2,1)}, u32[]{:S(2)}, u32[]{:S(2)}) collective-permute-start(bf16[272,1024]{1,0:T(8,128)(2,1)} %collective-permute-done.6.refs_1_), channel_id=1, source_target_pairs={{0,7},{1,0},{2,1},{3,2},{4,3},{5,4},{6,5},{7,6},{8,15},{9,8},{10,9... | collective-permute-start | bytes 1671176 | tf_op jit(solution)/shard_map/ppermute | solution.py:32
  63.5 16.1 %collective-permute-start.4 = (bf16[272,1024]{1,0:T(8,128)(2,1)}, bf16[272,1024]{1,0:T(8,128)(2,1)}, u32[]{:S(2)}, u32[]{:S(2)}) collective-permute-start(bf16[272,1024]{1,0:T(8,128)(2,1)} %collective-permute-done.3.refs_0_), channel_id=1, source_target_pairs={{0,1},{1,2},{2,3},{3,4},{4,5},{5,6},{6,7},{7,0},{8,9},{9,10},{10,1... | collective-permute-start | bytes 1671176 | tf_op jit(solution)/shard_map/ppermute | solution.py:32
  65.4 25.0 %collective-permute-start = (bf16[128,8192]{1,0:T(8,128)(2,1)}, bf16[128,8192]{1,0:T(8,128)(2,1)}, u32[]{:S(2)}, u32[]{:S(2)}) collective-permute-start(bf16[128,8192]{1,0:T(8,128)(2,1)} %bitcast.31), channel_id=1, source_target_pairs={{0,32},{32,0},{1,33},{33,1},{2,34},{34,2},{3,35},{35,3},{4,36},{36... | collective-permute-start | bytes 6291464 | tf_op jit(solution)/shard_map/ppermute | solution.py:36
  81.9 32.9 %all-to-all-start.2 = ((bf16[8,8,64,256]{3,2,1,0:T(8,128)(2,1)}), bf16[8,8,64,256]{3,2,1,0:T(8,128)(2,1)}, u32[]{:S(2)}, u32[]{:S(2)}) async-start(bf16[8,8,64,256]{3,2,1,0:T(8,128)(2,1)} %get-tuple-element.31.refs_0_.refs_4_), calls=%async_computation.2 | async-start | bytes 4194304 | tf_op jit(solution)/shard_map/all_to_all | solution.py:27
  120.4 6.9 %copy-start.6 = (bf16[64,512]{1,0:T(8,128)(2,1)S(1)}, bf16[64,512]{1,0:T(8,128)(2,1)}, u32[]{:S(2)}) copy-start(bf16[64,512]{1,0:T(8,128)(2,1)} %copy-done.5) | copy-start | bytes 196612
  120.4 36.2 %all-to-all-start.3 = ((bf16[8,8,8192]{2,1,0:T(8,128)(2,1)}), bf16[8,8,8192]{2,1,0:T(8,128)(2,1)S(1)}, u32[]{:S(2)}, u32[]{:S(2)}) async-start(bf16[8,8,8192]{2,1,0:T(8,128)(2,1)} %bitcast.35), calls=%async_computation.3 | async-start | bytes 2097152 | tf_op jit(solution)/shard_map/all_to_all | solution.py:27
  127.3 8.8 %collective-permute-start.10 = (bf16[64,512]{1,0:T(8,128)(2,1)S(1)}, bf16[64,512]{1,0:T(8,128)(2,1)S(1)}, u32[]{:S(2)}, u32[]{:S(2)}) collective-permute-start(bf16[64,512]{1,0:T(8,128)(2,1)S(1)} %copy-done.6), channel_id=1, source_target_pairs={{0,16},{8,24},{16,0},{24,8},{1,17},{9,25},{17,1},{25,9},{2,18},{10... | collective-permute-start | bytes 196616 | tf_op jit(solution)/shard_map/ppermute | solution.py:32
  129.9 6.2 %collective-permute-start.8 = (bf16[64,512]{1,0:T(8,128)(2,1)S(1)}, bf16[64,512]{1,0:T(8,128)(2,1)S(1)}, u32[]{:S(2)}, u32[]{:S(2)}) collective-permute-start(bf16[64,512]{1,0:T(8,128)(2,1)S(1)} %copy-done.6), channel_id=1, source_target_pairs={{0,24},{8,0},{16,8},{24,16},{1,25},{9,1},{17,9},{25,17},{2,26},{10... | collective-permute-start | bytes 196616 | tf_op jit(solution)/shard_map/ppermute | solution.py:32
  134.1 6.5 %collective-permute-start.9 = (bf16[64,512]{1,0:T(8,128)(2,1)S(1)}, bf16[64,512]{1,0:T(8,128)(2,1)S(1)}, u32[]{:S(2)}, u32[]{:S(2)}) collective-permute-start(bf16[64,512]{1,0:T(8,128)(2,1)S(1)} %copy-done.6), channel_id=1, source_target_pairs={{0,8},{8,16},{16,24},{24,0},{1,9},{9,17},{17,25},{25,1},{2,10},{10... | collective-permute-start | bytes 196616 | tf_op jit(solution)/shard_map/ppermute | solution.py:32
  141.3 12.3 %collective-permute-start.11 = (bf16[4,72,256]{2,1,0:T(8,128)(2,1)S(1)}, bf16[4,72,256]{2,1,0:T(8,128)(2,1)S(1)}, u32[]{:S(2)}, u32[]{:S(2)}) collective-permute-start(bf16[4,72,256]{2,1,0:T(8,128)(2,1)S(1)} %get-tuple-element.40), channel_id=1, source_target_pairs={{0,4},{1,5},{2,6},{3,7},{4,0},{5,1},{6,2},{7,3},{8,12},{9,13},{10,... | collective-permute-start | bytes 442376 | tf_op jit(solution)/shard_map/ppermute | solution.py:36
  156.6 37.0 %copy-start = (bf16[64,8192]{1,0:T(8,128)(2,1)S(1)}, bf16[64,8192]{1,0:T(8,128)(2,1)}, u32[]{:S(2)}) copy-start(bf16[64,8192]{1,0:T(8,128)(2,1)} %get-tuple-element.47.sum_ref) | copy-start | bytes 3145732
  157.7 32.7 %all-to-all-start.4 = ((bf16[8,8,8192]{2,1,0:T(8,128)(2,1)}), bf16[8,8,8192]{2,1,0:T(8,128)(2,1)S(1)}, u32[]{:S(2)}, u32[]{:S(2)}) async-start(bf16[8,8,8192]{2,1,0:T(8,128)(2,1)} %sums_above.1), calls=%async_computation.4 | async-start | bytes 2097152 | tf_op jit(solution)/shard_map/all_to_all | solution.py:27
  161.3 6.2 %collective-permute-start.12 = (bf16[2,72,256]{2,1,0:T(8,128)(2,1)S(1)}, bf16[2,72,256]{2,1,0:T(8,128)(2,1)S(1)}, u32[]{:S(2)}, u32[]{:S(2)}) collective-permute-start(bf16[2,72,256]{2,1,0:T(8,128)(2,1)S(1)} %get-tuple-element.42), channel_id=1, source_target_pairs={{0,2},{1,3},{2,0},{3,1},{4,6},{5,7},{6,4},{7,5},{8,10},{9,11},{10,... | collective-permute-start | bytes 221192 | tf_op jit(solution)/shard_map/ppermute | solution.py:36
  167.4 5.0 %collective-permute-start.13 = (bf16[1,72,256]{2,1,0:T(8,128)(2,1)S(1)}, bf16[1,72,256]{2,1,0:T(8,128)(2,1)S(1)}, u32[]{:S(2)}, u32[]{:S(2)}) collective-permute-start(bf16[1,72,256]{2,1,0:T(8,128)(2,1)S(1)} %get-tuple-element.44), channel_id=1, source_target_pairs={{0,1},{1,0},{2,3},{3,2},{4,5},{5,4},{6,7},{7,6},{8,9},{9,8},{10,11... | collective-permute-start | bytes 110600 | tf_op jit(solution)/shard_map/ppermute | solution.py:36
  172.5 23.3 %collective-permute-start.15 = (bf16[64,8192]{1,0:T(8,128)(2,1)}, bf16[64,8192]{1,0:T(8,128)(2,1)S(1)}, u32[]{:S(2)}, u32[]{:S(2)}) collective-permute-start(bf16[64,8192]{1,0:T(8,128)(2,1)} %get-tuple-element.46), channel_id=1, source_target_pairs={{0,32},{32,0},{1,33},{33,1},{2,34},{34,2},{3,35},{35,3},{4,36},{36... | collective-permute-start | bytes 3145736 | tf_op jit(solution)/shard_map/ppermute | solution.py:36
  190.4 5.4 %collective-permute-start.14 = (bf16[64,8192]{1,0:T(8,128)(2,1)S(1)}, bf16[64,8192]{1,0:T(8,128)(2,1)}, u32[]{:S(2)}, u32[]{:S(2)}) collective-permute-start(bf16[64,8192]{1,0:T(8,128)(2,1)S(1)} %bitcast.25), channel_id=1, source_target_pairs={{0,32},{32,0},{1,33},{33,1},{2,34},{34,2},{3,35},{35,3},{4,36},{36... | collective-permute-start | bytes 3145736 | tf_op jit(solution)/shard_map/ppermute | solution.py:36
  (5 other events, 10.6 us)
